TPU v7x, 256 devices: a whole 4x4x8 slice. The times are simulated.
256 devices in a mesh: dp: 32 (over z, y_hi, core), ctx: 8 (over x, y_lo).
Axes of the slice: x: 4, y: 4 (y_hi: 2, y_lo: 2; y = y_hi * 2 + y_lo), z: 8, core: 2. Of those that a mesh axis runs over, the one named last changes fastest.
Arguments:
- q_heads: bfloat16 [32, 1536, 2048], P('dp', 'ctx'), may hold values from -8 to 8
- keys: bfloat16 [32, 1536, 128], P('dp', 'ctx'), may hold values from -8 to 8
- values: bfloat16 [32, 1536, 128], P('dp', 'ctx'), may hold values from -6 to 6
- out_grad: bfloat16 [32, 1536, 2048], P('dp', 'ctx'), may hold values from -0.29882812 to 0.29882812
- hidden_in: bfloat16 [32, 1536, 16384], P('dp', 'ctx'), may hold values from -6 to 6
- doc_lengths: int32 [32, 8], P('dp'), may hold values from 1 to 576, 1536 in all within a row
- span_order: int32 [16], replicated, may hold values from 0 to 15, each once
- m_codes: int32 [16384, 256], P('dp'), may hold values from -127 to 127
- m_scales: float32 [2048], P('dp'), may hold values from 0.05 to 0.5
- v_codes: int32 [16384, 256], P('dp'), may hold values from 1 to 255
- v_scales: float32 [2048], P('dp'), may hold values from 0.05 to 1
Outputs:
- dq: bfloat16 [32, 1536, 2048], P('dp', 'ctx')
- update: float32 [16384, 256], P('dp')
- m_norm: float32 [16384, 256], P('dp')
- m_absmax: float32 [2048], P('dp')
- v_norm: float32 [16384, 256], P('dp')
- v_absmax: float32 [2048], P('dp')
Inputs may be any that keep to these rules, and one draw needn't show every extreme that they name: `doc_lengths`: each sequence's 8 lengths sum to 1536. `span_order`: each stored block names a different position block.
All inputs are finite; a program needn't handle non-finite values. Where the computation divides by a largest or mean magnitude, that divisor is 1e-20 or more.
Results may differ from a plain program's by a relative error of at most 0.0078.
Values may be sent and summed in bfloat16 or wider, within the bound.
A program may use at most 128 MiB of HBM per device.

v0:
```python
import math

import jax
import jax.numpy as jnp
from jax import lax
from jax.sharding import PartitionSpec as P

BLOCK = 2048
STEP = 10


def positions(order, span, total):
    rows = jnp.arange(total, dtype=jnp.int32)
    slot = rows // span
    match = slot[:, None] == jnp.arange(order.shape[0], dtype=jnp.int32)[None, :]
    first = jnp.sum(jnp.where(match, order[None, :], 0), axis=1)
    return first * span + rows % span


def documents(pos, lengths):
    ends = jnp.cumsum(lengths)
    return jnp.sum((pos[:, None] >= ends[None, :]).astype(jnp.int32), axis=1)


def adam_blocks(grad, m_codes, m_scales, v_codes, v_scales):
    shape = grad.shape
    g_blocks = grad.reshape(-1, BLOCK)
    m_old = m_codes.reshape(-1, BLOCK).astype(jnp.float32) / 127.0 * m_scales[:, None]
    v_old = v_codes.reshape(-1, BLOCK).astype(jnp.float32) / 255.0 * v_scales[:, None]
    moment = 0.9 * m_old + 0.1 * g_blocks
    second = 0.95 * v_old + 0.05 * g_blocks * g_blocks
    update = moment / (1.0 - 0.9**STEP) / (jnp.sqrt(second / (1.0 - 0.95**STEP)) + 1e-08)
    m_absmax = jnp.max(jnp.abs(moment), axis=1)
    v_absmax = jnp.max(second, axis=1)
    m_norm = moment / (m_absmax[:, None] + 1e-06)
    v_norm = second / (v_absmax[:, None] + 1e-06)
    return (update.reshape(shape), m_norm.reshape(shape), m_absmax, v_norm.reshape(shape), v_absmax)


def contract_rows(left, right):
    return lax.dot_general(
        left, right, (((0,), (0,)), ((), ())), preferred_element_type=jnp.float32
    )


def contract_cols(left, right):
    return lax.dot_general(
        left, right, (((1,), (1,)), ((), ())), preferred_element_type=jnp.float32
    )


def shards(
    q_heads,
    keys,
    values,
    out_grad,
    hidden_in,
    doc_lengths,
    span_order,
    m_codes,
    m_scales,
    v_codes,
    v_scales,
):
    rows = q_heads.shape[1]
    head_dim = keys.shape[2]
    heads_width = q_heads.shape[2]
    nheads = heads_width // head_dim
    scale = 1.0 / math.sqrt(head_dim)
    total = rows * lax.axis_size("ctx")
    key_all, value_all = (
        lax.all_gather(keys[0], "ctx", axis=0, tiled=True),
        lax.all_gather(values[0], "ctx", axis=0, tiled=True),
    )
    pos = positions(span_order, rows // 2, total)
    doc = documents(pos, doc_lengths[0])
    first_row = lax.axis_index("ctx") * rows
    query_pos = lax.dynamic_slice_in_dim(pos, first_row, rows)
    query_doc = lax.dynamic_slice_in_dim(doc, first_row, rows)
    queries = q_heads[0].reshape(rows * nheads, head_dim)
    grads_out = out_grad[0].reshape(rows * nheads, head_dim)
    width = min(512, total)
    nblocks = total // width
    blocks = (
        key_all.reshape(nblocks, width, head_dim),
        value_all.reshape(nblocks, width, head_dim),
        pos.reshape(nblocks, width),
        doc.reshape(nblocks, width),
    )

    def block_masks(key_pos, key_doc):
        small = (key_pos[None, :] <= query_pos[:, None]) & (key_doc[None, :] == query_doc[:, None])
        wide = jnp.broadcast_to(small[:, None, :], (rows, nheads, width)).reshape(
            rows * nheads, width
        )
        return (small, wide)

    def forward_terms(carry, block):
        key_block, value_block, key_pos, key_doc = block
        small, wide = block_masks(key_pos, key_doc)
        top, denom, weighted = carry
        scores = contract_cols(queries, key_block) * scale
        dprob = contract_cols(grads_out, value_block)
        new_top = jnp.maximum(top, jnp.max(jnp.where(wide, scores, -1e30), axis=1, keepdims=True))
        expo = jnp.where(wide, jnp.exp(scores - new_top), 0.0)
        factor = jnp.exp(top - new_top)
        result = (
            new_top,
            denom * factor + jnp.sum(expo, axis=1, keepdims=True),
            weighted * factor + jnp.sum(expo * dprob, axis=1, keepdims=True),
        )
        return (result, None)

    column = jnp.zeros((rows * nheads, 1), jnp.float32)
    start_state = (column - 1e30, column, column)
    (top, denom, weighted), unused = lax.scan(forward_terms, start_state, blocks)
    delta = weighted / denom

    def backward_terms(accum, block):
        key_block, value_block, key_pos, key_doc = block
        small, wide = block_masks(key_pos, key_doc)
        acc = accum
        scores = contract_cols(queries, key_block) * scale
        dprob = contract_cols(grads_out, value_block)
        prob = jnp.where(wide, jnp.exp(scores - top), 0.0) / denom
        prob_low = prob.astype(jnp.bfloat16)
        dscore = (prob * (dprob - delta)).astype(jnp.bfloat16)
        acc = acc + jnp.dot(dscore, key_block, preferred_element_type=jnp.float32)
        dkey = contract_rows(dscore, queries) * scale
        dvalue = contract_rows(prob_low, grads_out)
        return (acc, jnp.concatenate([dkey, dvalue], axis=1))

    dq_sum, pieces = lax.scan(
        backward_terms, jnp.zeros((rows * nheads, head_dim), jnp.float32), blocks
    )
    dq = (dq_sum * scale).reshape(1, rows, heads_width).astype(jnp.bfloat16)
    partial_grads = pieces.reshape(total, 2 * head_dim)
    own = lax.psum_scatter(partial_grads, "ctx", scatter_dimension=0, tiled=True)
    own_low = own.astype(jnp.bfloat16)
    layer_in = hidden_in[0]
    grad = lax.psum_scatter(contract_rows(layer_in, own_low), "dp", scatter_dimension=0, tiled=True)
    grad = lax.psum(grad, "ctx")
    update, m_norm, m_absmax, v_norm, v_absmax = adam_blocks(
        grad, m_codes, m_scales, v_codes, v_scales
    )
    return (dq, update, m_norm, m_absmax, v_norm, v_absmax)


def solution(mesh):
    in_specs = (
        P("dp", "ctx", None),
        P("dp", "ctx", None),
        P("dp", "ctx", None),
        P("dp", "ctx", None),
        P("dp", "ctx", None),
        P("dp", None),
        P(),
        P("dp", None),
        P("dp"),
        P("dp", None),
        P("dp"),
    )
    out_specs = (
        P("dp", "ctx", None),
        P("dp", None),
        P("dp", None),
        P("dp"),
        P("dp", None),
        P("dp"),
    )
    return jax.shard_map(shards, mesh=mesh, in_specs=in_specs, out_specs=out_specs, check_vma=False)
```

profile of v0, /device:TPU:8, one launch (start us, length us, event | category | flops | bytes accessed | tf_op | source)
XLA Modules:
  0.0 547.1 jit_solution(15692817767166467675)
XLA Ops:
  11.0 29.2 %all-gather = bf16[1,1536,128]{2,1,0:T(8,128)(2,1)S(1)} all-gather(bf16[1,192,128]{2,1,0:T(8,128)(2,1)} %param.16), channel_id=2, replica_groups=mesh['dp'=32,'ctx'=8] {'ctx'}, dimensions={1}, use_global_device_ids=true | all-gather | bytes 442368 | tf_op jit(solution)/shard_map/all_gather | solution.py:72
  41.6 30.8 %all-gather.1 = bf16[1,1536,128]{2,1,0:T(8,128)(2,1)} all-gather(bf16[1,192,128]{2,1,0:T(8,128)(2,1)} %param.17), channel_id=3, replica_groups=mesh['dp'=32,'ctx'=8] {'ctx'}, dimensions={1}, use_global_device_ids=true | all-gather | bytes 442368 | tf_op jit(solution)/shard_map/all_gather | solution.py:73
  72.8 46.8 %while.28 = (s32[]{:T(128)}, f32[3072,1]{0,1:T(1,128)}, f32[3072,1]{0,1:T(1,128)}, f32[3072,1]{0,1:T(1,128)}, s32[3,512]{1,0:T(4,128)}, /*index=5*/s32[192]{0:T(...) while((s32[]{:T(128)}, f32[3072,1]{0,1:T(1,128)}, ...), condition=%wide.region_7.8_spmd.clone, body=%wide.region_3.7_spmd.clone.sunk | while | flops 824497152 | bytes 55990092 | solution.py:116
  74.8 1.7 copy.45
  76.5 3.9 fusion.79
  80.4 5.2 fusion.81
  89.9 1.7 copy.45
  91.6 3.9 fusion.79
  96.2 5.2 fusion.81
  105.7 1.7 copy.45
  107.4 3.8 fusion.79
  112.0 5.2 fusion.81
  121.0 55.8 %while.29 = (s32[]{:T(128)}, f32[3072,128]{1,0:T(8,128)}, f32[3,512,256]{2,1,0:T(8,128)}, s32[3,512]{1,0:T(4,128)}, s32[192]{0:T(256)S(1)}, /*index=5*/s32[3,512...) while((s32[]{:T(128)}, f32[3072,128]{1,0:T(8,128)}, ...), condition=%wide.region_9.10_spmd.clone, body=%wide.region_8.9_spmd.clone.sunk | while | flops 2027126784 | bytes 108267456 | solution.py:133
  124.8 1.9 fusion.94
  126.8 2.9 fusion.95
  129.8 2.2 convolution_add_fusion.2
  133.1 2.3 fusion.96
  135.4 2.3 convolution_multiply_fusion.2
  143.1 1.9 fusion.94
  145.1 2.9 fusion.95
  148.1 3.8 convolution_add_fusion.2
  151.8 2.3 fusion.96
  154.2 2.3 convolution_multiply_fusion.2
  161.9 1.9 fusion.94
  163.8 2.9 fusion.95
  166.8 3.8 convolution_add_fusion.2
  170.6 2.3 fusion.96
  172.9 2.3 convolution_multiply_fusion.2
  176.8 48.1 %reduce-scatter.3.cloned.1.call-done = f32[192,256]{1,0:T(8,128)} async-done(((f32[1536,256]{1,0:T(8,128)}), f32[192,256]{1,0:T(8,128)}) %reduce-scatter.3.cloned.1.call-update) | async-done | bytes 196624 | tf_op jit(solution)/shard_map/reduce_scatter | solution.py:138
  224.9 11.0 %convolution_bitcast_fusion = f32[16384,256]{0,1:T(8,128)} fusion(bf16[1,192,16384]{2,1,0:T(8,128)(2,1)} %param.19, f32[192,256]{1,0:T(8,128)} %reduce-scatter.3.cloned.1.call-done), kind=kOutput, calls=%fused_computation.49 | convolution fusion | flops 1610661888 | bytes 23265280 | tf_op jit(solution)/shard_map/dot_general | solution.py:41
  236.0 219.7 %reduce-scatter.5.cloned.1.call-done = f32[512,256]{0,1:T(8,128)} async-done(((f32[16384,256]{0,1:T(8,128)}), f32[512,256]{0,1:T(8,128)}) %reduce-scatter.5.cloned.1.call-update) | async-done | bytes 524304 | tf_op jit(solution)/shard_map/reduce_scatter | solution.py:141
  457.9 77.3 %all-reduce.2.cloned.1.call-done = f32[512,256]{0,1:T(8,128)} async-done(((f32[512,256]{0,1:T(8,128)}), f32[512,256]{0,1:T(8,128)}) %all-reduce.2.cloned.1.call-update) | async-done | bytes 524304 | tf_op jit(solution)/shard_map/psum | solution.py:142
  (197 shorter events, 45.8 us)
Async XLA Ops:
  7.2 65.3 %copy-start.10 = (bf16[1,192,2048]{2,1,0:T(8,128)(2,1)S(1)}, bf16[1,192,2048]{2,1,0:T(8,128)(2,1)}, u32[]{:S(2)}) copy-start(bf16[1,192,2048]{2,1,0:T(8,128)(2,1)} %param.18) | copy-start | bytes 2359300
  7.2 217.7 %reduce-scatter.3.cloned.1.call-start = ((), (), s32[]{:S(2)}) async-start(), calls=%async_computation.2 | async-start | bytes 1769472 | tf_op jit(solution)/shard_map/reduce_scatter | solution.py:138
  80.4 5.2 copy-start
  96.2 5.2 copy-start
  112.0 5.2 copy-start
  121.0 5.8 %copy-start.4 = (bf16[3072,128]{1,0:T(8,128)(2,1)}, bf16[3072,128]{1,0:T(8,128)(2,1)S(1)}, u32[]{:S(2)}) copy-start(bf16[3072,128]{1,0:T(8,128)(2,1)S(1)} %get-tuple-element.577) | copy-start | bytes 2359300 | tf_op jit(solution)/shard_map/while
  121.0 5.8 %copy-start.6 = (bf16[3072,128]{1,0:T(8,128)(2,1)}, bf16[3072,128]{1,0:T(8,128)(2,1)S(1)}, u32[]{:S(2)}) copy-start(bf16[3072,128]{1,0:T(8,128)(2,1)S(1)} %get-tuple-element.581) | copy-start | bytes 2359300 | tf_op jit(solution)/shard_map/while
  121.0 3.8 copy-start.9
  121.0 3.8 copy-start.16
  126.8 3.0 copy-start.1
  129.7 3.4 copy-start.2
  139.3 5.8 %copy-start.4 = (bf16[3072,128]{1,0:T(8,128)(2,1)}, bf16[3072,128]{1,0:T(8,128)(2,1)S(1)}, u32[]{:S(2)}) copy-start(bf16[3072,128]{1,0:T(8,128)(2,1)S(1)} %get-tuple-element.577) | copy-start | bytes 2359300 | tf_op jit(solution)/shard_map/while
  139.3 5.8 %copy-start.6 = (bf16[3072,128]{1,0:T(8,128)(2,1)}, bf16[3072,128]{1,0:T(8,128)(2,1)S(1)}, u32[]{:S(2)}) copy-start(bf16[3072,128]{1,0:T(8,128)(2,1)S(1)} %get-tuple-element.581) | copy-start | bytes 2359300 | tf_op jit(solution)/shard_map/while
  139.3 3.8 copy-start.9
  139.3 3.8 copy-start.16
  145.1 3.0 copy-start.1
  148.1 3.8 copy-start.2
  158.0 5.8 %copy-start.4 = (bf16[3072,128]{1,0:T(8,128)(2,1)}, bf16[3072,128]{1,0:T(8,128)(2,1)S(1)}, u32[]{:S(2)}) copy-start(bf16[3072,128]{1,0:T(8,128)(2,1)S(1)} %get-tuple-element.577) | copy-start | bytes 2359300 | tf_op jit(solution)/shard_map/while
  158.0 5.8 %copy-start.6 = (bf16[3072,128]{1,0:T(8,128)(2,1)}, bf16[3072,128]{1,0:T(8,128)(2,1)S(1)}, u32[]{:S(2)}) copy-start(bf16[3072,128]{1,0:T(8,128)(2,1)S(1)} %get-tuple-element.581) | copy-start | bytes 2359300 | tf_op jit(solution)/shard_map/while
  158.0 3.8 copy-start.9
  158.0 3.8 copy-start.16
  163.8 3.0 copy-start.1
  166.8 3.8 copy-start.2
  176.8 279.0 %reduce-scatter.5.cloned.1.call-start = ((), (), s32[]{:S(2)}) async-start(), calls=%async_computation.3 | async-start | bytes 17301504 | tf_op jit(solution)/shard_map/reduce_scatter | solution.py:141
  235.9 219.8 %copy-start.3 = (f32[3072,128]{1,0:T(8,128)S(1)}, f32[3072,128]{1,0:T(8,128)}, u32[]{:S(2)}) copy-start(f32[3072,128]{1,0:T(8,128)} %get-tuple-element.146) | copy-start | bytes 4718596
  235.9 221.2 %copy-start.21 = (f32[64]{0:T(128)S(1)}, f32[64]{0:T(128)}, u32[]{:S(2)}) copy-start(f32[64]{0:T(128)} %param.23) | copy-start | bytes 772
  236.0 221.3 %copy-start.11 = (s32[512,256]{1,0:T(8,128)S(1)}, s32[512,256]{1,0:T(8,128)}, u32[]{:S(2)}) copy-start(s32[512,256]{1,0:T(8,128)} %param.22) | copy-start | bytes 1572868
  236.0 221.5 %copy-start.22 = (f32[64]{0:T(128)S(1)}, f32[64]{0:T(128)}, u32[]{:S(2)}) copy-start(f32[64]{0:T(128)} %param.25) | copy-start | bytes 772
  236.0 221.7 %copy-start.12 = (s32[512,256]{1,0:T(8,128)S(1)}, s32[512,256]{1,0:T(8,128)}, u32[]{:S(2)}) copy-start(s32[512,256]{1,0:T(8,128)} %param.24) | copy-start | bytes 1572868
  236.0 299.2 %all-reduce.2.cloned.1.call-start = ((), (), s32[]{:S(2)}) async-start(), calls=%async_computation.4 | async-start | bytes 1048576 | tf_op jit(solution)/shard_map/psum | solution.py:142
  536.7 3.9 copy-start.19
  537.1 3.5 copy-start.20
  (24 other events, 33.0 us)
Sparse Core Ops, SparseCore 0:
  176.9 47.9 reduce-scatter.2
  236.1 219.6 reduce-scatter.4
  458.6 76.5 all-reduce.1
where the time goes:
time: 550 us; the launch traced here: 547 us
  waiting for transfers between devices  345 us (63%)
  matrix products  76.2 us (14%)
  blocking collectives  60 us (11%)
  local copies, waits for them, and re-layouts  33.6 us (6%)
  other arithmetic  17.2 us (3%)
  between operations  14 us (3%)
    reduce_scatter x1, waiting for transfers between devices, shards(): lax.psum_scatter(contract_rows(layer_in, own_low), 'dp', scatter_dimensio...  220 us
    psum x1, waiting for transfers between devices, shards(): grad = lax.psum(grad, 'ctx')  77.3 us
    reduce_scatter x1, waiting for transfers between devices, shards(): lax.psum_scatter(partial_grads, 'ctx', scatter_dimension=0, tiled=True)  48.1 us
    dot_general x12, matrix products, contract_cols(): lax.dot_general(left, right, (((1,), (1,)), ((), ())), preferred_element_...  41.6 us
    all_gather x1, blocking collectives, shards(): lax.all_gather(values[0], 'ctx', axis=0, tiled=True)  30.8 us
    all_gather x1, blocking collectives, shards(): lax.all_gather(keys[0], 'ctx', axis=0, tiled=True)  29.2 us
    dot_general x7, matrix products, contract_rows(): lax.dot_general(left, right, (((0,), (0,)), ((), ())), preferred_element_...  24.8 us
  transfers between devices with their start and end apart: 3, of which 3 were waited for; matrix products, arithmetic and copies ran while one was open for 0% of the time, Pallas kernels for 0%

commit v1 on v0

--- a/solution.py
+++ b/solution.py
@@ -18,7 +18,8 @@
 
 
 def documents(pos, lengths):
-    ends = jnp.cumsum(lengths)
+    index = jnp.arange(lengths.shape[0], dtype=jnp.int32)
+    ends = jnp.sum(jnp.where(index[None, :] <= index[:, None], lengths[None, :], 0), axis=1)
     return jnp.sum((pos[:, None] >= ends[None, :]).astype(jnp.int32), axis=1)
 
 

time: 550 us -> 550 us (level)
  no operation moved by 1% of the time
where the time goes in v1:
time: 550 us; the launch traced here: 547 us
  waiting for transfers between devices  345 us (63%)
  matrix products  76.2 us (14%)
  blocking collectives  60 us (11%)
  local copies, waits for them, and re-layouts  33.6 us (6%)
  other arithmetic  17.1 us (3%)
  between operations  14 us (3%)
    reduce_scatter x1, waiting for transfers between devices, shards(): lax.psum_scatter(contract_rows(layer_in, own_low), 'dp', scatter_dimensio...  220 us
    psum x1, waiting for transfers between devices, shards(): grad = lax.psum(grad, 'ctx')  77.3 us
    reduce_scatter x1, waiting for transfers between devices, shards(): lax.psum_scatter(partial_grads, 'ctx', scatter_dimension=0, tiled=True)  48.1 us
    dot_general x12, matrix products, contract_cols(): lax.dot_general(left, right, (((1,), (1,)), ((), ())), preferred_element_...  41.6 us
    all_gather x1, blocking collectives, shards(): lax.all_gather(values[0], 'ctx', axis=0, tiled=True)  30.8 us
    all_gather x1, blocking collectives, shards(): lax.all_gather(keys[0], 'ctx', axis=0, tiled=True)  29.2 us
    dot_general x7, matrix products, contract_rows(): lax.dot_general(left, right, (((0,), (0,)), ((), ())), preferred_element_...  24.8 us
  transfers between devices with their start and end apart: 3, of which 3 were waited for; matrix products, arithmetic and copies ran while one was open for 0% of the time, Pallas kernels for 0%

profile of v1, /device:TPU:8, one launch (start us, length us, event | category | flops | bytes accessed | tf_op | source)
XLA Modules:
  0.0 547.0 jit_solution(25946978486925844)
XLA Ops:
  10.9 29.2 %all-gather = bf16[1,1536,128]{2,1,0:T(8,128)(2,1)S(1)} all-gather(bf16[1,192,128]{2,1,0:T(8,128)(2,1)} %param.16), channel_id=2, replica_groups=mesh['dp'=32,'ctx'=8] {'ctx'}, dimensions={1}, use_global_device_ids=true | all-gather | bytes 442368 | tf_op jit(solution)/shard_map/all_gather | solution.py:73
  41.6 30.8 %all-gather.1 = bf16[1,1536,128]{2,1,0:T(8,128)(2,1)} all-gather(bf16[1,192,128]{2,1,0:T(8,128)(2,1)} %param.17), channel_id=3, replica_groups=mesh['dp'=32,'ctx'=8] {'ctx'}, dimensions={1}, use_global_device_ids=true | all-gather | bytes 442368 | tf_op jit(solution)/shard_map/all_gather | solution.py:74
  72.8 46.8 %while.28 = (s32[]{:T(128)}, f32[3072,1]{0,1:T(1,128)}, f32[3072,1]{0,1:T(1,128)}, f32[3072,1]{0,1:T(1,128)}, s32[3,512]{1,0:T(4,128)}, /*index=5*/s32[192]{0:T(...) while((s32[]{:T(128)}, f32[3072,1]{0,1:T(1,128)}, ...), condition=%wide.region_7.8_spmd.clone, body=%wide.region_3.7_spmd.clone.sunk | while | flops 824497152 | bytes 55990092 | solution.py:117
  74.7 1.7 copy.45
  76.4 3.9 fusion.79
  80.3 5.2 fusion.81
  89.9 1.7 copy.45
  91.6 3.9 fusion.79
  96.1 5.2 fusion.81
  105.7 1.7 copy.45
  107.4 3.8 fusion.79
  112.0 5.2 fusion.81
  120.9 55.8 %while.29 = (s32[]{:T(128)}, f32[3072,128]{1,0:T(8,128)}, f32[3,512,256]{2,1,0:T(8,128)}, s32[3,512]{1,0:T(4,128)}, s32[192]{0:T(256)S(1)}, /*index=5*/s32[3,512...) while((s32[]{:T(128)}, f32[3072,128]{1,0:T(8,128)}, ...), condition=%wide.region_9.10_spmd.clone, body=%wide.region_8.9_spmd.clone.sunk | while | flops 2027126784 | bytes 108267456 | solution.py:134
  124.7 1.9 fusion.94
  126.7 2.9 fusion.95
  129.7 2.2 convolution_add_fusion.2
  133.0 2.3 fusion.96
  135.4 2.3 convolution_multiply_fusion.2
  143.1 1.9 fusion.94
  145.0 2.9 fusion.95
  148.0 3.8 convolution_add_fusion.2
  151.8 2.3 fusion.96
  154.1 2.3 convolution_multiply_fusion.2
  161.8 1.9 fusion.94
  163.8 2.9 fusion.95
  166.7 3.8 convolution_add_fusion.2
  170.5 2.3 fusion.96
  172.8 2.3 convolution_multiply_fusion.2
  176.8 48.1 %reduce-scatter.3.cloned.1.call-done = f32[192,256]{1,0:T(8,128)} async-done(((f32[1536,256]{1,0:T(8,128)}), f32[192,256]{1,0:T(8,128)}) %reduce-scatter.3.cloned.1.call-update) | async-done | bytes 196624 | tf_op jit(solution)/shard_map/reduce_scatter | solution.py:139
  224.9 11.0 %convolution_bitcast_fusion = f32[16384,256]{0,1:T(8,128)} fusion(bf16[1,192,16384]{2,1,0:T(8,128)(2,1)} %param.19, f32[192,256]{1,0:T(8,128)} %reduce-scatter.3.cloned.1.call-done), kind=kOutput, calls=%fused_computation.49 | convolution fusion | flops 1610661888 | bytes 23265280 | tf_op jit(solution)/shard_map/dot_general | solution.py:42
  236.0 219.7 %reduce-scatter.5.cloned.1.call-done = f32[512,256]{0,1:T(8,128)} async-done(((f32[16384,256]{0,1:T(8,128)}), f32[512,256]{0,1:T(8,128)}) %reduce-scatter.5.cloned.1.call-update) | async-done | bytes 524304 | tf_op jit(solution)/shard_map/reduce_scatter | solution.py:142
  457.9 77.3 %all-reduce.2.cloned.1.call-done = f32[512,256]{0,1:T(8,128)} async-done(((f32[512,256]{0,1:T(8,128)}), f32[512,256]{0,1:T(8,128)}) %all-reduce.2.cloned.1.call-update) | async-done | bytes 524304 | tf_op jit(solution)/shard_map/psum | solution.py:143
  (197 shorter events, 45.8 us)
Async XLA Ops:
  7.2 65.2 %copy-start.10 = (bf16[1,192,2048]{2,1,0:T(8,128)(2,1)S(1)}, bf16[1,192,2048]{2,1,0:T(8,128)(2,1)}, u32[]{:S(2)}) copy-start(bf16[1,192,2048]{2,1,0:T(8,128)(2,1)} %param.18) | copy-start | bytes 2359300
  7.2 217.7 %reduce-scatter.3.cloned.1.call-start = ((), (), s32[]{:S(2)}) async-start(), calls=%async_computation.2 | async-start | bytes 1769472 | tf_op jit(solution)/shard_map/reduce_scatter | solution.py:139
  80.3 5.2 copy-start
  96.1 5.2 copy-start
  112.0 5.2 copy-start
  120.9 5.8 %copy-start.4 = (bf16[3072,128]{1,0:T(8,128)(2,1)}, bf16[3072,128]{1,0:T(8,128)(2,1)S(1)}, u32[]{:S(2)}) copy-start(bf16[3072,128]{1,0:T(8,128)(2,1)S(1)} %get-tuple-element.577) | copy-start | bytes 2359300 | tf_op jit(solution)/shard_map/while
  120.9 5.8 %copy-start.6 = (bf16[3072,128]{1,0:T(8,128)(2,1)}, bf16[3072,128]{1,0:T(8,128)(2,1)S(1)}, u32[]{:S(2)}) copy-start(bf16[3072,128]{1,0:T(8,128)(2,1)S(1)} %get-tuple-element.581) | copy-start | bytes 2359300 | tf_op jit(solution)/shard_map/while
  120.9 3.8 copy-start.9
  120.9 3.8 copy-start.16
  126.7 3.0 copy-start.1
  129.7 3.4 copy-start.2
  139.2 5.8 %copy-start.4 = (bf16[3072,128]{1,0:T(8,128)(2,1)}, bf16[3072,128]{1,0:T(8,128)(2,1)S(1)}, u32[]{:S(2)}) copy-start(bf16[3072,128]{1,0:T(8,128)(2,1)S(1)} %get-tuple-element.577) | copy-start | bytes 2359300 | tf_op jit(solution)/shard_map/while
  139.2 5.8 %copy-start.6 = (bf16[3072,128]{1,0:T(8,128)(2,1)}, bf16[3072,128]{1,0:T(8,128)(2,1)S(1)}, u32[]{:S(2)}) copy-start(bf16[3072,128]{1,0:T(8,128)(2,1)S(1)} %get-tuple-element.581) | copy-start | bytes 2359300 | tf_op jit(solution)/shard_map/while
  139.2 3.8 copy-start.9
  139.2 3.8 copy-start.16
  145.0 3.0 copy-start.1
  148.0 3.8 copy-start.2
  158.0 5.8 %copy-start.4 = (bf16[3072,128]{1,0:T(8,128)(2,1)}, bf16[3072,128]{1,0:T(8,128)(2,1)S(1)}, u32[]{:S(2)}) copy-start(bf16[3072,128]{1,0:T(8,128)(2,1)S(1)} %get-tuple-element.577) | copy-start | bytes 2359300 | tf_op jit(solution)/shard_map/while
  158.0 5.8 %copy-start.6 = (bf16[3072,128]{1,0:T(8,128)(2,1)}, bf16[3072,128]{1,0:T(8,128)(2,1)S(1)}, u32[]{:S(2)}) copy-start(bf16[3072,128]{1,0:T(8,128)(2,1)S(1)} %get-tuple-element.581) | copy-start | bytes 2359300 | tf_op jit(solution)/shard_map/while
  158.0 3.8 copy-start.9
  158.0 3.8 copy-start.16
  163.8 3.0 copy-start.1
  166.7 3.8 copy-start.2
  176.7 279.0 %reduce-scatter.5.cloned.1.call-start = ((), (), s32[]{:S(2)}) async-start(), calls=%async_computation.3 | async-start | bytes 17301504 | tf_op jit(solution)/shard_map/reduce_scatter | solution.py:142
  235.9 219.8 %copy-start.3 = (f32[3072,128]{1,0:T(8,128)S(1)}, f32[3072,128]{1,0:T(8,128)}, u32[]{:S(2)}) copy-start(f32[3072,128]{1,0:T(8,128)} %get-tuple-element.146) | copy-start | bytes 4718596
  235.9 221.2 %copy-start.21 = (f32[64]{0:T(128)S(1)}, f32[64]{0:T(128)}, u32[]{:S(2)}) copy-start(f32[64]{0:T(128)} %param.23) | copy-start | bytes 772
  235.9 221.3 %copy-start.11 = (s32[512,256]{1,0:T(8,128)S(1)}, s32[512,256]{1,0:T(8,128)}, u32[]{:S(2)}) copy-start(s32[512,256]{1,0:T(8,128)} %param.22) | copy-start | bytes 1572868
  235.9 221.5 %copy-start.22 = (f32[64]{0:T(128)S(1)}, f32[64]{0:T(128)}, u32[]{:S(2)}) copy-start(f32[64]{0:T(128)} %param.25) | copy-start | bytes 772
  235.9 221.7 %copy-start.12 = (s32[512,256]{1,0:T(8,128)S(1)}, s32[512,256]{1,0:T(8,128)}, u32[]{:S(2)}) copy-start(s32[512,256]{1,0:T(8,128)} %param.24) | copy-start | bytes 1572868
  235.9 299.2 %all-reduce.2.cloned.1.call-start = ((), (), s32[]{:S(2)}) async-start(), calls=%async_computation.4 | async-start | bytes 1048576 | tf_op jit(solution)/shard_map/psum | solution.py:143
  536.6 3.9 copy-start.19
  537.0 3.5 copy-start.20
  (24 other events, 33.0 us)
Sparse Core Ops, SparseCore 0:
  176.8 47.9 reduce-scatter.2
  236.0 219.6 reduce-scatter.4
  458.5 76.5 all-reduce.1

commit v2 on v0

v2 whole, which is shorter than its diff:
```python
import functools
import math

import jax
import jax.numpy as jnp
from jax import lax
from jax.experimental import pallas as pl
from jax.experimental.pallas import tpu as pltpu
from jax.sharding import PartitionSpec as P

STEP = 10
SPAN = 96
WINDOW = 7
HEAD = 128
GROUP = 4
NGROUPS = 4
Z_ORDER = (4, 3, 5, 2, 6, 1, 7, 0)
F32 = jnp.float32
BF16 = jnp.bfloat16
WIRE = jnp.float32
MESH = pl.DeviceIdType.MESH


def remote(src, dst, send, recv, device):
    return pltpu.make_async_remote_copy(
        src_ref=src, dst_ref=dst, send_sem=send, recv_sem=recv, device_id=device, device_id_type=MESH
    )


def greet(devices):
    barrier = pltpu.get_barrier_semaphore()
    for device in devices:
        pl.semaphore_signal(barrier, inc=1, device_id=device, device_id_type=MESH)
    pl.semaphore_wait(barrier, len(devices))


def gather_kernel(k_ref, v_ref, kall, vall, own_sem, send, recv):
    dp, ctx = lax.axis_index("dp"), lax.axis_index("ctx")
    rows = k_ref.shape[0]
    mine = pl.ds(pl.multiple_of(ctx * rows, rows), rows)
    own = [
        pltpu.make_async_copy(k_ref, kall.at[mine], own_sem.at[0]),
        pltpu.make_async_copy(v_ref, vall.at[mine], own_sem.at[1]),
    ]
    for copy in own:
        copy.start()
    peers = [(dp, lax.rem(ctx + o, 8)) for o in range(1, 8)]
    greet(peers)
    copies = []
    for o in (4, 3, 5, 2, 6, 1, 7):
        for which, (src, dst) in enumerate(((k_ref, kall), (v_ref, vall))):
            copy = remote(src, dst.at[mine], send.at[which, o], recv.at[which, o], peers[o - 1])
            copy.start()
            copies.append((copy, which, o, src, dst))
    for copy in own:
        copy.wait()
    for copy, which, o, src, dst in copies:
        copy.wait_send()
        theirs = pl.ds(pl.multiple_of(lax.rem(ctx + 8 - o, 8) * rows, rows), rows)
        remote(src, dst.at[theirs], send.at[which, o], recv.at[which, o], peers[o - 1]).wait_recv()


def gather(keys, values):
    rows, width = keys.shape
    shape = jax.ShapeDtypeStruct((8 * rows, width), keys.dtype)
    any_space = pl.BlockSpec(memory_space=pl.ANY)
    return pl.pallas_call(
        gather_kernel,
        out_shape=[shape, shape],
        in_specs=[any_space] * 2,
        out_specs=[any_space] * 2,
        scratch_shapes=[
            pltpu.SemaphoreType.DMA((2,)),
            pltpu.SemaphoreType.DMA((2, 8)),
            pltpu.SemaphoreType.DMA((2, 8)),
        ],
        compiler_params=pltpu.CompilerParams(collective_id=0, has_side_effects=True),
        name="gather_kv",
    )(keys, values)


def dot_t(left, right):
    return lax.dot_general(left, right, (((1,), (1,)), ((), ())), preferred_element_type=F32)


def attention_kernel(
    order, lens, q_ref, g_ref, kall, vall, dq_ref, dkv_ref,
    inverse, k7, v7, k7t, bias, s_scr, d_scr, p_scr, ds_scr, dk7, dv7, acc,
):
    ctx = lax.axis_index("ctx")
    scale = 1.0 / math.sqrt(HEAD)
    factor = scale * math.log2(math.e)
    width = GROUP * SPAN
    for s in range(16):
        inverse[order[s]] = s
    acc[...] = jnp.zeros_like(acc)

    def query_block(qb, carry):
        place = order[ctx * 2 + qb]
        first = place - (WINDOW - 1)
        stored = [pl.multiple_of(inverse[jnp.maximum(first + r, 0)] * SPAN, SPAN) for r in range(WINDOW)]
        for r in range(WINDOW):
            part = pl.ds(r * SPAN, SPAN)
            k7[part, :] = kall[pl.ds(stored[r], SPAN), :]
            v7[part, :] = vall[pl.ds(stored[r], SPAN), :]
        k7t[...] = k7[...].astype(F32).T.astype(BF16)
        lane = lax.broadcasted_iota(jnp.int32, (1, width), 1)
        head = jnp.zeros_like(lane)
        for h in range(1, GROUP):
            head = head + (lane >= h * SPAN).astype(jnp.int32)
        query_pos = place * SPAN + lane - head * SPAN
        begin = jnp.zeros_like(lane)
        end = jnp.int32(0)
        for k in range(8):
            end = end + lens[0, k]
            begin = jnp.where(query_pos >= end, end, begin)
        for r in range(WINDOW):
            key_pos = (first + r) * SPAN + lax.broadcasted_iota(jnp.int32, (SPAN, width), 0)
            allowed = (key_pos <= query_pos) & (key_pos >= begin)
            bias[pl.ds(r * SPAN, SPAN), :] = jnp.where(allowed, 0.0, -1e30)
        dk7[...] = jnp.zeros_like(dk7)
        dv7[...] = jnp.zeros_like(dv7)
        rows = pl.ds(pl.multiple_of(qb * SPAN, SPAN), SPAN)

        def head_group(grp, carry):
            lanes = [pl.ds(pl.multiple_of(grp * (GROUP * HEAD), GROUP * HEAD) + h * HEAD, HEAD) for h in range(GROUP)]
            queries = jnp.concatenate([q_ref[rows, c] for c in lanes], axis=0)
            cots = jnp.concatenate([g_ref[rows, c] for c in lanes], axis=0)
            top = jnp.full((8, width), -3e38, F32)
            for r in range(WINDOW):
                part = pl.ds(r * SPAN, SPAN)
                scores = dot_t(k7[part, :], queries) + bias[part, :]
                s_scr[part, :] = scores
                d_scr[part, :] = dot_t(v7[part, :], cots)
                top = jnp.maximum(top, jnp.max(scores.reshape(SPAN // 8, 8, width), axis=0))
            top = jnp.max(top, axis=0, keepdims=True)
            denom = jnp.zeros((8, width), F32)
            weighted = jnp.zeros((8, width), F32)
            for r in range(WINDOW):
                part = pl.ds(r * SPAN, SPAN)
                expo = jnp.exp2((s_scr[part, :] - top) * factor)
                s_scr[part, :] = expo
                denom = denom + jnp.sum(expo.reshape(SPAN // 8, 8, width), axis=0)
                weighted = weighted + jnp.sum((expo * d_scr[part, :]).reshape(SPAN // 8, 8, width), axis=0)
            inv = 1.0 / jnp.sum(denom, axis=0, keepdims=True)
            delta = jnp.sum(weighted, axis=0, keepdims=True) * inv
            for r in range(WINDOW):
                part = pl.ds(r * SPAN, SPAN)
                prob = s_scr[part, :] * inv
                p_scr[part, :] = prob.astype(BF16)
                ds_scr[part, :] = (prob * (d_scr[part, :] - delta)).astype(BF16)
            dv7[...] += jnp.dot(p_scr[...], cots, preferred_element_type=F32)
            dk7[...] += jnp.dot(ds_scr[...], queries, preferred_element_type=F32)
            dq = (jnp.dot(k7t[...], ds_scr[...], preferred_element_type=F32) * scale).T.astype(BF16)
            for h in range(GROUP):
                dq_ref[rows, lanes[h]] = dq[h * SPAN : (h + 1) * SPAN, :]
            return carry

        lax.fori_loop(0, 16 // GROUP, head_group, 0)
        for r in range(WINDOW):
            part = pl.ds(r * SPAN, SPAN)
            target = pl.ds(stored[r], SPAN)
            acc[target, 0:HEAD] += dk7[part, :] * scale
            acc[target, HEAD : 2 * HEAD] += dv7[part, :]
        return carry

    lax.fori_loop(0, 2, query_block, 0)
    dkv_ref[...] = acc[...].astype(WIRE)


def attention(order, lens, queries, cots, kall, vall):
    keys = WINDOW * SPAN
    width = GROUP * SPAN
    smem = pl.BlockSpec(memory_space=pltpu.SMEM)
    vmem = pl.BlockSpec(memory_space=pltpu.VMEM)
    return pl.pallas_call(
        attention_kernel,
        out_shape=[
            jax.ShapeDtypeStruct(queries.shape, BF16),
            jax.ShapeDtypeStruct((kall.shape[0], 2 * HEAD), WIRE),
        ],
        in_specs=[smem, smem, vmem, vmem, vmem, vmem],
        out_specs=[vmem, vmem],
        scratch_shapes=[
            pltpu.SMEM((16,), jnp.int32),
            pltpu.VMEM((keys, HEAD), BF16),
            pltpu.VMEM((keys, HEAD), BF16),
            pltpu.VMEM((HEAD, keys), BF16),
            pltpu.VMEM((keys, width), F32),
            pltpu.VMEM((keys, width), F32),
            pltpu.VMEM((keys, width), F32),
            pltpu.VMEM((keys, width), BF16),
            pltpu.VMEM((keys, width), BF16),
            pltpu.VMEM((keys, HEAD), F32),
            pltpu.VMEM((keys, HEAD), F32),
            pltpu.VMEM((kall.shape[0], 2 * HEAD), F32),
        ],
        compiler_params=pltpu.CompilerParams(vmem_limit_bytes=40 * 2**20),
        name="attention_backward",
    )(order, lens, queries, cots, kall, vall)


def reduce_kernel(
    dkv_ref, hid, out_ref,
    held, dkv_in, dkv2, dkvt,
    first, one_in1, two_in1, second, one_in2, two_in2, z_out, z_in, total, gathered,
    hid_own, hid_send, hid_recv, dkv_send, dkv_recv, pair_send, pair_recv,
    send1, recv1, send2, recv2, z_send, z_recv, ag_send, ag_recv,
):
    dp, ctx = lax.axis_index("dp"), lax.axis_index("ctx")
    x, ylo = ctx // 2, lax.rem(ctx, 2)
    z, yhi, core = dp // 4, lax.rem(dp // 2, 2), lax.rem(dp, 2)
    y = yhi * 2 + ylo
    rows = hid.shape[0]

    def at(xx, yy, zz):
        return (zz * 4 + (yy // 2) * 2 + core, xx * 2 + lax.rem(yy, 2))

    x_up, x_down = lax.rem(x + 1, 4), lax.rem(x + 3, 4)
    y_up, y_down = lax.rem(y + 1, 4), lax.rem(y + 3, 4)
    pair = (dp + 1 - 2 * core, ctx)
    ctx_peers = [(dp, lax.rem(ctx + o, 8)) for o in range(1, 8)]
    z_peers = [at(x, y, lax.rem(z + o, 8)) for o in range(1, 8)]
    across = at(x, lax.rem(y + 3 + 2 * ylo, 4), z)

    def columns(slot, c):
        o, yh = Z_ORDER[slot // 2], slot % 2
        block = lax.rem(z + o, 8) * 4 + yh * 2 + c
        return pl.ds(pl.multiple_of(block * 512, 512), 512)

    own = [
        pltpu.make_async_copy(hid.at[:, columns(s, core)], held.at[s, pl.ds(0, rows)], hid_own.at[s])
        for s in range(16)
    ]
    for copy in own:
        copy.start()
    greet([*ctx_peers, *z_peers, pair, across])
    dkv_copies = []
    for o in (4, 3, 5, 2, 6, 1, 7):
        block = pl.ds(pl.multiple_of(lax.rem(ctx + o, 8) * rows, rows), rows)
        copy = remote(dkv_ref.at[block], dkv_in.at[o], dkv_send.at[o], dkv_recv.at[o], ctx_peers[o - 1])
        copy.start()
        dkv_copies.append(copy)
    swaps = []
    for s in range(16):
        copy = remote(
            hid.at[:, columns(s, 1 - core)], held.at[s, pl.ds(rows, rows)], hid_send.at[s], hid_recv.at[s], pair
        )
        copy.start()
        swaps.append(copy)
    for copy in dkv_copies:
        copy.wait()
    total_dkv = dkv_ref[pl.ds(pl.multiple_of(ctx * rows, rows), rows), :].astype(F32)
    for o in range(1, 8):
        total_dkv = total_dkv + dkv_in[o].astype(F32)
    dkv2[pl.ds(0, rows), :] = total_dkv.astype(BF16)
    swap = remote(dkv2.at[pl.ds(0, rows)], dkv2.at[pl.ds(rows, rows)], pair_send, pair_recv, pair)
    swap.start()
    swap.wait()
    dkvt[...] = dkv2[...].astype(F32).T.astype(BF16)

    axes = (
        ((x, at(x_up, y, z), at(x_down, y, z)), (y, at(x, y_up, z), at(x, y_down, z))),
        ((y, at(x, y_up, z), at(x, y_down, z)), (x, at(x_up, y, z), at(x_down, y, z))),
    )
    pending = []

    def ring(stage, part, g):
        place, up, down = axes[part][stage]
        units = 8 if stage == 0 else 2
        half = units // 2
        low, high = pl.ds(0, half), pl.ds(half, half)
        data = (first if stage == 0 else second).at[part, g]
        in1 = (one_in1 if stage == 0 else one_in2).at[part, g]
        in2 = (two_in1 if stage == 0 else two_in2).at[part, g]
        send = (send1 if stage == 0 else send2).at[part, g]
        recv = (recv1 if stage == 0 else recv2).at[part, g]
        after, before, opposite = lax.rem(place + 1, 4), lax.rem(place + 3, 4), lax.rem(place + 2, 4)
        pairs = {
            "a": (data.at[opposite, low], in1.at[0], up),
            "b": (data.at[opposite, high], in1.at[1], down),
            "c": (data.at[after, high], in2.at[0, high], up),
            "d": (data.at[before, low], in2.at[1, low], down),
            "e": (data.at[after, low], in2.at[0, low], up),
            "f": (data.at[before, high], in2.at[1, high], down),
        }

        def copy(name):
            k = "abcdef".index(name)
            src, dst, device = pairs[name]
            return remote(src, dst, send.at[k], recv.at[k], device)

        return dict(
            copy=copy, data=data, in1=in1, in2=in2, low=low, high=high, after=after, before=before, place=place
        )

    def begin(stage, part, g):
        r = ring(stage, part, g)
        for name in "abcd":
            copy = r["copy"](name)
            copy.start()
            pending.append(copy)

    def relay(stage, part, g):
        r = ring(stage, part, g)
        data = r["data"]
        for k, (arrived, sent, place, half) in enumerate((("a", "e", "after", "low"), ("b", "f", "before", "high"))):
            here = (r[place], r[half])
            r["copy"](arrived).wait_recv()
            data[here] = (data[here].astype(F32) + r["in1"][k].astype(F32)).astype(WIRE)
            copy = r["copy"](sent)
            copy.start()
            pending.append(copy)

    def finish(stage, part, g):
        r = ring(stage, part, g)
        for name in "cdef":
            r["copy"](name).wait_recv()
        return r["data"][r["place"]].astype(F32) + r["in2"][0].astype(F32) + r["in2"][1].astype(F32)

    def compute(g):
        for s in range(4 * g, 4 * g + 4):
            own[s].wait()
            swaps[s].wait()

        def block(k, carry):
            j, yh = k // 2, lax.rem(k, 2)
            product = jnp.dot(dkvt[...], held[4 * g + k], preferred_element_type=F32).astype(WIRE)
            for xx in range(4):
                for yl in range(2):
                    r0 = (xx * 2 + yl) * 32
                    yy = yh * 2 + yl
                    first[0, g, xx, yy * 2 + j] = product[r0 : r0 + 32, 0:256]
                    first[1, g, yy, xx * 2 + j] = product[r0 : r0 + 32, 256:512]
            return carry

        lax.fori_loop(0, 4, block, 0)
        for part in range(2):
            begin(0, part, g)

    def middle(g):
        for part in range(2):
            done = finish(0, part, g)
            for t in range(4):
                second[part, g, t] = done[2 * t : 2 * t + 2].astype(WIRE)
            begin(1, part, g)

    def last(g):
        for part in range(2):
            done = finish(1, part, g)
            for j in range(2):
                z_out[2 * g + j, part] = done[j].astype(WIRE)
        for j in range(2):
            o = Z_ORDER[2 * g + j]
            if o:
                copy = remote(z_out.at[2 * g + j], z_in.at[o], z_send.at[o], z_recv.at[o], z_peers[o - 1])
                copy.start()
                pending.append(copy)

    for tick in range(-1, NGROUPS + 4):
        if tick + 1 < NGROUPS:
            compute(tick + 1)
        if 0 <= tick - 3 < NGROUPS:
            last(tick - 3)
        if 0 <= tick - 2 < NGROUPS:
            for part in range(2):
                relay(1, part, tick - 2)
        if 0 <= tick - 1 < NGROUPS:
            middle(tick - 1)
        if 0 <= tick < NGROUPS:
            for part in range(2):
                relay(0, part, tick)

    sums = z_out[Z_ORDER.index(0)].astype(F32)
    for o in (1, 7, 2, 6, 3, 5, 4):
        remote(z_out.at[0], z_in.at[o], z_send.at[o], z_recv.at[o], z_peers[o - 1]).wait_recv()
        sums = sums + z_in[o].astype(F32)
    total[...] = sums
    copies = []
    for o in (4, 3, 5, 2, 6, 1, 7):
        copy = remote(total, gathered.at[o], ag_send.at[o], ag_recv.at[o], ctx_peers[o - 1])
        copy.start()
        copies.append(copy)
    out_ref[ctx] = sums
    for copy in pending:
        copy.wait_send()
    for copy in copies:
        copy.wait()
    for o in range(1, 8):
        out_ref[lax.rem(ctx + 8 - o, 8)] = gathered[o]


def reduce_gradient(dkv, hidden):
    rows = hidden.shape[0]
    dma = pltpu.SemaphoreType.DMA
    unit = (32, 256)
    return pl.pallas_call(
        reduce_kernel,
        out_shape=jax.ShapeDtypeStruct((8, 2, *unit), F32),
        in_specs=[pl.BlockSpec(memory_space=pltpu.VMEM), pl.BlockSpec(memory_space=pl.ANY)],
        out_specs=pl.BlockSpec(memory_space=pltpu.VMEM),
        scratch_shapes=[
            pltpu.VMEM((16, 2 * rows, 512), BF16),
            pltpu.VMEM((8, rows, 256), WIRE),
            pltpu.VMEM((2 * rows, 256), BF16),
            pltpu.VMEM((256, 2 * rows), BF16),
            pltpu.VMEM((2, NGROUPS, 4, 8, *unit), WIRE),
            pltpu.VMEM((2, NGROUPS, 2, 4, *unit), WIRE),
            pltpu.VMEM((2, NGROUPS, 2, 8, *unit), WIRE),
            pltpu.VMEM((2, NGROUPS, 4, 2, *unit), WIRE),
            pltpu.VMEM((2, NGROUPS, 2, 1, *unit), WIRE),
            pltpu.VMEM((2, NGROUPS, 2, 2, *unit), WIRE),
            pltpu.VMEM((8, 2, *unit), WIRE),
            pltpu.VMEM((8, 2, *unit), WIRE),
            pltpu.VMEM((2, *unit), F32),
            pltpu.VMEM((8, 2, *unit), F32),
            dma((16,)), dma((16,)), dma((16,)), dma((8,)), dma((8,)), dma, dma,
            dma((2, NGROUPS, 6)), dma((2, NGROUPS, 6)), dma((2, NGROUPS, 6)), dma((2, NGROUPS, 6)),
            dma((8,)), dma((8,)), dma((8,)), dma((8,)),
        ],
        compiler_params=pltpu.CompilerParams(
            collective_id=1, has_side_effects=True, vmem_limit_bytes=48 * 2**20
        ),
        name="project_and_reduce",
    )(dkv, hidden)


def adam_kernel(grad_t, m_codes, m_scales, v_codes, v_scales, update, m_norm, m_absmax, v_norm, v_absmax, grad):
    for part in range(2):
        grad[pl.ds(part * 256, 256), :] = grad_t[:, part].reshape(256, 256).T

    def block(b, carry):
        rows = pl.ds(pl.multiple_of(b * 8, 8), 8)
        g = grad[rows, :]
        m = 0.9 * (m_codes[rows, :].astype(F32) * (m_scales[b] * (1.0 / 127.0))) + 0.1 * g
        v = 0.95 * (v_codes[rows, :].astype(F32) * (v_scales[b] * (1.0 / 255.0))) + 0.05 * g * g
        update[rows, :] = m * (1.0 / (1.0 - 0.9**STEP)) / (jnp.sqrt(v * (1.0 / (1.0 - 0.95**STEP))) + 1e-08)
        m_top = jnp.max(jnp.abs(m))
        v_top = jnp.max(v)
        m_absmax[b] = m_top
        v_absmax[b] = v_top
        m_norm[rows, :] = m / (m_top + 1e-06)
        v_norm[rows, :] = v / (v_top + 1e-06)
        return carry

    lax.fori_loop(0, 64, block, 0, unroll=8)


def adam(grad_t, m_codes, m_scales, v_codes, v_scales):
    smem = pl.BlockSpec(memory_space=pltpu.SMEM)
    vmem = pl.BlockSpec(memory_space=pltpu.VMEM)
    big = jax.ShapeDtypeStruct(m_codes.shape, F32)
    small = jax.ShapeDtypeStruct(m_scales.shape, F32)
    return pl.pallas_call(
        adam_kernel,
        out_shape=[big, big, small, big, small],
        in_specs=[vmem, vmem, smem, vmem, smem],
        out_specs=[vmem, vmem, smem, vmem, smem],
        scratch_shapes=[pltpu.VMEM(m_codes.shape, F32)],
        compiler_params=pltpu.CompilerParams(vmem_limit_bytes=32 * 2**20),
        name="adam",
    )(grad_t, m_codes, m_scales, v_codes, v_scales)


def shards(
    q_heads, keys, values, out_grad, hidden_in, doc_lengths, span_order, m_codes, m_scales, v_codes, v_scales
):
    kall, vall = gather(keys[0], values[0])
    dq, dkv = attention(span_order, doc_lengths, q_heads[0], out_grad[0], kall, vall)
    grad_t = reduce_gradient(dkv, hidden_in[0])
    update, m_norm, m_absmax, v_norm, v_absmax = adam(grad_t, m_codes, m_scales, v_codes, v_scales)
    return (dq[None], update, m_norm, m_absmax, v_norm, v_absmax)


def solution(mesh):
    in_specs = (
        P("dp", "ctx", None),
        P("dp", "ctx", None),
        P("dp", "ctx", None),
        P("dp", "ctx", None),
        P("dp", "ctx", None),
        P("dp", None),
        P(),
        P("dp", None),
        P("dp"),
        P("dp", None),
        P("dp"),
    )
    out_specs = (
        P("dp", "ctx", None),
        P("dp", None),
        P("dp", None),
        P("dp"),
        P("dp", None),
        P("dp"),
    )
    return jax.shard_map(shards, mesh=mesh, in_specs=in_specs, out_specs=out_specs, check_vma=False)
```

time: 550 us -> 133 us (0.24)
  waiting for transfers between devices: 345 us -> 0 us
  Pallas kernels: 0 us -> 126 us
  matrix products: 76.2 us -> 0 us
  blocking collectives: 60 us -> 0 us
  local copies, waits for them, and re-layouts: 33.6 us -> 5.58 us
  other arithmetic: 17.2 us -> 0 us
  between operations: 14 us -> 0.71 us
    reduce_scatter x2 -> x0, waiting for transfers between devices: 268 us -> none  [the longest x1 220 us: shards(): lax.psum_scatter(contract_rows(layer_in, own_low), 'dp', scatter_dimensio...]
    pallas_call x0 -> x4, Pallas kernels: none -> 126 us  [the longest x1 92.6 us: reduce_gradient(): pl.pallas_call(reduce_kernel, out_shape=jax.ShapeDtypeStruct((8, 2, *unit...]
    psum x1 -> x0, waiting for transfers between devices: 77.3 us -> none  [shards(): grad = lax.psum(grad, 'ctx')]
    dot_general x22 -> x0, matrix products: 76.2 us -> none  [the longest x12 41.6 us: contract_cols(): lax.dot_general(left, right, (((1,), (1,)), ((), ())), preferred_element_...]
    all_gather x2 -> x0, blocking collectives: 60 us -> none  [the longest x1 30.8 us: shards(): lax.all_gather(values[0], 'ctx', axis=0, tiled=True)]
    reshape x7 -> x0, local copies, waits for them, and re-layouts: 10.7 us -> none  [the longest x6 10.1 us: block_masks(): jnp.broadcast_to(small[:, None, :], (rows, nheads, width))]
    reduce_sum x5 -> x0, other arithmetic: 5.83 us -> none  [the longest x3 4.94 us: forward_terms(): jnp.sum(expo, axis=1, keepdims=True)]
  transfers between devices with their start and end apart: 3 -> 0, of which waited for: 3 -> 0; matrix products, arithmetic and copies ran while one was open for 0% -> 0% of each run, Pallas kernels for 0% -> 0%
where the time goes in v2:
time: 133 us; the launch traced here: 132 us
  Pallas kernels  126 us (95%)
  local copies, waits for them, and re-layouts  5.58 us (4%)
    pallas_call x1, Pallas kernels, reduce_gradient(): pl.pallas_call(reduce_kernel, out_shape=jax.ShapeDtypeStruct((8, 2, *unit...  92.6 us
    pallas_call x1, Pallas kernels, attention(): pl.pallas_call(attention_kernel, out_shape=[jax.ShapeDtypeStruct(queries....  15.3 us
    pallas_call x1, Pallas kernels, gather(): pl.pallas_call(gather_kernel, out_shape=[shape, shape], in_specs=[any_spa...  14.7 us
    unnamed x20, local copies, waits for them, and re-layouts  5.58 us
    pallas_call x1, Pallas kernels, adam(): pl.pallas_call(adam_kernel, out_shape=[big, big, small, big, small], in_s...  3.39 us

profile of v2, /device:TPU:8, one launch (start us, length us, event | category | flops | bytes accessed | tf_op | source)
XLA Modules:
  0.0 132.3 jit_solution(12806393656130571486)
XLA Ops:
  0.6 0.0 copy-start.7
  0.6 0.0 copy-start.6
  0.7 14.7 %gather_kv.1 = (bf16[1536,128]{1,0:T(8,128)(2,1)}, bf16[1536,128]{1,0:T(8,128)(2,1)}) custom-call(bf16[192,128]{1,0:T(8,128)(2,1)} %bitcast.9, bf16[192,128]{1,0:T(8,128)(2,1)} %bitcast.10), custom_call_target="tpu_custom_call" | custom-call | tf_op jit(solution)/shard_map/gather_kv/pallas_call | solution.py:67
  15.4 0.0 copy-start
  15.4 1.1 copy-done
  16.5 0.0 copy-start.1
  16.5 1.1 copy-done.1
  17.7 0.0 copy-start.4
  17.7 1.0 copy-done.4
  18.7 0.0 copy-start.5
  18.7 1.0 copy-done.5
  19.6 0.0 copy-start.8
  19.7 0.7 copy-done.8
  20.3 0.0 copy-start.9
  20.3 0.7 copy-done.9
  21.0 0.0 copy-start.2
  21.0 0.0 copy-start.3
  21.0 15.3 %attention_backward.1 = (bf16[192,2048]{1,0:T(8,128)(2,1)}, f32[1536,256]{1,0:T(8,128)S(1)}) custom-call(s32[16]{0:T(128)S(1)} %copy-done.8, s32[1,8]{1,0:T(1,128)S(1)} %copy-done.9, bf16[192,2048]{1,0:T(8,128)(2,1)S(1)} %bitcast.6, bf16[192,2048]{1,0:T(8,128)(2,1)S(1)} %bitcast.7, bf16[1536,128]{1,0:T(8,128)(2,1)S(1)} %copy-done.4, ...), custom_call_target="tpu_custom_call" | custom-call | tf_op jit(solution)/shard_map/attention_backward/pallas_call | solution.py:176
  36.2 92.6 %project_and_reduce.1.grad_t = f32[8,2,32,256]{3,2,1,0:T(8,128)S(1)} custom-call(f32[1536,256]{1,0:T(8,128)S(1)} %get-tuple-element.18.dkv_ref, bf16[192,16384]{1,0:T(8,128)(2,1)} %bitcast.8), custom_call_target="tpu_custom_call" | custom-call | tf_op jit(solution)/shard_map/project_and_reduce/pallas_call | solution.py:397
  128.9 0.0 copy-done.7
  128.9 0.0 copy-done.6
  128.9 0.0 copy-done.2
  128.9 0.0 copy-done.3
  128.9 3.4 %adam.1 = (f32[512,256]{1,0:T(8,128)}, f32[512,256]{1,0:T(8,128)}, f32[64]{0:T(128)}, f32[512,256]{1,0:T(8,128)}, f32[64]{0:T(128)}) custom-call(f32[8,2,32,256]{3,2,1,0:T(8,128)S(1)} %project_and_reduce.1.grad_t, s32[512,256]{1,0:T(8,128)S(1)} %copy-done.2, f32[64]{0:T(128)S(1)} %copy-done.6, s32[512,256]{1,0:T(8,128)S(1)} %copy-done.3, f32[64]{0:T(128)S(1)} %copy-done.7), custom_call_target="tpu_custom_call" | custom-call | tf_op jit(solution)/shard_map/adam/pallas_call | solution.py:454
Async XLA Ops:
  0.6 128.2 %copy-start.7 = (f32[64]{0:T(128)S(1)}, f32[64]{0:T(128)}, u32[]{:S(2)}) copy-start(f32[64]{0:T(128)} %v_scales.1) | copy-start | bytes 772
  0.6 128.2 %copy-start.6 = (f32[64]{0:T(128)S(1)}, f32[64]{0:T(128)}, u32[]{:S(2)}) copy-start(f32[64]{0:T(128)} %m_scales.1) | copy-start | bytes 772
  15.4 1.1 copy-start
  16.5 1.1 copy-start.1
  17.7 1.0 copy-start.4
  18.7 1.0 copy-start.5
  19.6 0.7 copy-start.8
  20.3 0.7 copy-start.9
  21.0 107.9 %copy-start.2 = (s32[512,256]{1,0:T(8,128)S(1)}, s32[512,256]{1,0:T(8,128)}, u32[]{:S(2)}) copy-start(s32[512,256]{1,0:T(8,128)} %m_codes.1) | copy-start | bytes 1572868
  21.0 107.9 %copy-start.3 = (s32[512,256]{1,0:T(8,128)S(1)}, s32[512,256]{1,0:T(8,128)}, u32[]{:S(2)}) copy-start(s32[512,256]{1,0:T(8,128)} %v_codes.1) | copy-start | bytes 1572868

commit v3 on v2

--- a/solution.py
+++ b/solution.py
@@ -14,10 +14,10 @@
 HEAD = 128
 GROUP = 4
 NGROUPS = 4
+FAR_FIRST = (4, 3, 5, 2, 6, 1, 7)
 Z_ORDER = (4, 3, 5, 2, 6, 1, 7, 0)
 F32 = jnp.float32
 BF16 = jnp.bfloat16
-WIRE = jnp.float32
 MESH = pl.DeviceIdType.MESH
 
 
@@ -32,6 +32,23 @@
     for device in devices:
         pl.semaphore_signal(barrier, inc=1, device_id=device, device_id_type=MESH)
     pl.semaphore_wait(barrier, len(devices))
+
+
+def encode(values, message):
+    rows = values.shape[0]
+    top = jnp.max(jnp.abs(values), axis=0, keepdims=True)
+    power = jnp.ceil(jnp.log2(jnp.maximum(top, 1e-30)))
+    codes = jnp.round(values * (jnp.exp2(-power) * 32000.0))
+    message[pl.ds(0, rows), :] = codes.astype(jnp.int32).astype(jnp.int16)
+    head = jnp.broadcast_to(power, (16, values.shape[1]))
+    message[pl.ds(rows, 16), :] = head.astype(jnp.int32).astype(jnp.int16)
+
+
+def decode(message):
+    rows = message.shape[0] - 16
+    power = message[pl.ds(rows, 16), :].astype(jnp.int32).astype(F32)[0:1, :]
+    codes = message[pl.ds(0, rows), :].astype(jnp.int32).astype(F32)
+    return codes * (jnp.exp2(power) * (1.0 / 32000.0))
 
 
 def gather_kernel(k_ref, v_ref, kall, vall, own_sem, send, recv):
@@ -165,7 +182,13 @@
         return carry
 
     lax.fori_loop(0, 2, query_block, 0)
-    dkv_ref[...] = acc[...].astype(WIRE)
+    own = 2 * SPAN
+
+    def write(c, carry):
+        encode(acc[pl.ds(pl.multiple_of(c * own, own), own), :], dkv_ref.at[c])
+        return carry
+
+    lax.fori_loop(0, 8, write, 0)
 
 
 def attention(order, lens, queries, cots, kall, vall):
@@ -177,7 +200,7 @@
         attention_kernel,
         out_shape=[
             jax.ShapeDtypeStruct(queries.shape, BF16),
-            jax.ShapeDtypeStruct((kall.shape[0], 2 * HEAD), WIRE),
+            jax.ShapeDtypeStruct((8, 2 * SPAN + 16, 2 * HEAD), jnp.int16),
         ],
         in_specs=[smem, smem, vmem, vmem, vmem, vmem],
         out_specs=[vmem, vmem],
@@ -202,8 +225,7 @@
 
 def reduce_kernel(
     dkv_ref, hid, out_ref,
-    held, dkv_in, dkv2, dkvt,
-    first, one_in1, two_in1, second, one_in2, two_in2, z_out, z_in, total, gathered,
+    held, dkv_in, dkv2, dkvt, first, out1, in1, second, out2, in2, z_out, z_in, ag_out, ag_in,
     hid_own, hid_send, hid_recv, dkv_send, dkv_recv, pair_send, pair_recv,
     send1, recv1, send2, recv2, z_send, z_recv, ag_send, ag_recv,
 ):
@@ -216,8 +238,8 @@
     def at(xx, yy, zz):
         return (zz * 4 + (yy // 2) * 2 + core, xx * 2 + lax.rem(yy, 2))
 
-    x_up, x_down = lax.rem(x + 1, 4), lax.rem(x + 3, 4)
-    y_up, y_down = lax.rem(y + 1, 4), lax.rem(y + 3, 4)
+    x_ring = (x, at(lax.rem(x + 1, 4), y, z), at(lax.rem(x + 3, 4), y, z))
+    y_ring = (y, at(x, lax.rem(y + 1, 4), z), at(x, lax.rem(y + 3, 4), z))
     pair = (dp + 1 - 2 * core, ctx)
     ctx_peers = [(dp, lax.rem(ctx + o, 8)) for o in range(1, 8)]
     z_peers = [at(x, y, lax.rem(z + o, 8)) for o in range(1, 8)]
@@ -236,9 +258,10 @@
         copy.start()
     greet([*ctx_peers, *z_peers, pair, across])
     dkv_copies = []
-    for o in (4, 3, 5, 2, 6, 1, 7):
-        block = pl.ds(pl.multiple_of(lax.rem(ctx + o, 8) * rows, rows), rows)
-        copy = remote(dkv_ref.at[block], dkv_in.at[o], dkv_send.at[o], dkv_recv.at[o], ctx_peers[o - 1])
+    for o in FAR_FIRST:
+        copy = remote(
+            dkv_ref.at[lax.rem(ctx + o, 8)], dkv_in.at[o], dkv_send.at[o], dkv_recv.at[o], ctx_peers[o - 1]
+        )
         copy.start()
         dkv_copies.append(copy)
     swaps = []
@@ -250,73 +273,62 @@
         swaps.append(copy)
     for copy in dkv_copies:
         copy.wait()
-    total_dkv = dkv_ref[pl.ds(pl.multiple_of(ctx * rows, rows), rows), :].astype(F32)
+    total_dkv = decode(dkv_ref.at[ctx])
     for o in range(1, 8):
-        total_dkv = total_dkv + dkv_in[o].astype(F32)
+        total_dkv = total_dkv + decode(dkv_in.at[o])
     dkv2[pl.ds(0, rows), :] = total_dkv.astype(BF16)
     swap = remote(dkv2.at[pl.ds(0, rows)], dkv2.at[pl.ds(rows, rows)], pair_send, pair_recv, pair)
     swap.start()
     swap.wait()
     dkvt[...] = dkv2[...].astype(F32).T.astype(BF16)
 
-    axes = (
-        ((x, at(x_up, y, z), at(x_down, y, z)), (y, at(x, y_up, z), at(x, y_down, z))),
-        ((y, at(x, y_up, z), at(x, y_down, z)), (x, at(x_up, y, z), at(x_down, y, z))),
-    )
+    rings = ((x_ring, y_ring), (y_ring, x_ring))
+    stages = ((first, out1, in1, send1, recv1, 4), (second, out2, in2, send2, recv2, 1))
     pending = []
 
-    def ring(stage, part, g):
-        place, up, down = axes[part][stage]
-        units = 8 if stage == 0 else 2
-        half = units // 2
-        low, high = pl.ds(0, half), pl.ds(half, half)
-        data = (first if stage == 0 else second).at[part, g]
-        in1 = (one_in1 if stage == 0 else one_in2).at[part, g]
-        in2 = (two_in1 if stage == 0 else two_in2).at[part, g]
-        send = (send1 if stage == 0 else send2).at[part, g]
-        recv = (recv1 if stage == 0 else recv2).at[part, g]
+    def piece(stage, part, g, place, high):
+        data, half = stages[stage][0], stages[stage][5]
+        return data.at[part, g, place, pl.ds(half * high, half)]
+
+    def flat(value):
+        return value.reshape(-1, 128)
+
+    def copy_of(stage, part, g, k):
+        data, out, into, send, recv, half = stages[stage]
+        up = k % 2 == 0
+        device = rings[part][stage][1 if up else 2]
+        return remote(out.at[part, g, k], into.at[part, g, k], send.at[part, g, k], recv.at[part, g, k], device)
+
+    def post(stage, part, g, k, value):
+        encode(value, stages[stage][1].at[part, g, k])
+        copy = copy_of(stage, part, g, k)
+        copy.start()
+        pending.append(copy)
+
+    def arrived(stage, part, g, k):
+        copy_of(stage, part, g, k).wait_recv()
+        return decode(stages[stage][2].at[part, g, k])
+
+    def begin(stage, part, g):
+        place = rings[part][stage][0]
         after, before, opposite = lax.rem(place + 1, 4), lax.rem(place + 3, 4), lax.rem(place + 2, 4)
-        pairs = {
-            "a": (data.at[opposite, low], in1.at[0], up),
-            "b": (data.at[opposite, high], in1.at[1], down),
-            "c": (data.at[after, high], in2.at[0, high], up),
-            "d": (data.at[before, low], in2.at[1, low], down),
-            "e": (data.at[after, low], in2.at[0, low], up),
-            "f": (data.at[before, high], in2.at[1, high], down),
-        }
-
-        def copy(name):
-            k = "abcdef".index(name)
-            src, dst, device = pairs[name]
-            return remote(src, dst, send.at[k], recv.at[k], device)
-
-        return dict(
-            copy=copy, data=data, in1=in1, in2=in2, low=low, high=high, after=after, before=before, place=place
-        )
-
-    def begin(stage, part, g):
-        r = ring(stage, part, g)
-        for name in "abcd":
-            copy = r["copy"](name)
-            copy.start()
-            pending.append(copy)
+        for k, (owner, high) in enumerate(((opposite, 0), (opposite, 1), (after, 1), (before, 0))):
+            post(stage, part, g, k, flat(piece(stage, part, g, owner, high)[...]))
 
     def relay(stage, part, g):
-        r = ring(stage, part, g)
-        data = r["data"]
-        for k, (arrived, sent, place, half) in enumerate((("a", "e", "after", "low"), ("b", "f", "before", "high"))):
-            here = (r[place], r[half])
-            r["copy"](arrived).wait_recv()
-            data[here] = (data[here].astype(F32) + r["in1"][k].astype(F32)).astype(WIRE)
-            copy = r["copy"](sent)
-            copy.start()
-            pending.append(copy)
+        place = rings[part][stage][0]
+        after, before = lax.rem(place + 1, 4), lax.rem(place + 3, 4)
+        for k, (owner, high) in enumerate(((after, 0), (before, 1))):
+            value = arrived(stage, part, g, k) + flat(piece(stage, part, g, owner, high)[...])
+            post(stage, part, g, 4 + k, value)
 
     def finish(stage, part, g):
-        r = ring(stage, part, g)
-        for name in "cdef":
-            r["copy"](name).wait_recv()
-        return r["data"][r["place"]].astype(F32) + r["in2"][0].astype(F32) + r["in2"][1].astype(F32)
+        place = rings[part][stage][0]
+        low = arrived(stage, part, g, 3) + arrived(stage, part, g, 4)
+        high = arrived(stage, part, g, 2) + arrived(stage, part, g, 5)
+        low = low + flat(piece(stage, part, g, place, 0)[...])
+        high = high + flat(piece(stage, part, g, place, 1)[...])
+        return low, high
 
     def compute(g):
         for s in range(4 * g, 4 * g + 4):
@@ -325,13 +337,14 @@
 
         def block(k, carry):
             j, yh = k // 2, lax.rem(k, 2)
-            product = jnp.dot(dkvt[...], held[4 * g + k], preferred_element_type=F32).astype(WIRE)
+            product = jnp.dot(dkvt[...], held[4 * g + k], preferred_element_type=F32)
             for xx in range(4):
                 for yl in range(2):
                     r0 = (xx * 2 + yl) * 32
                     yy = yh * 2 + yl
-                    first[0, g, xx, yy * 2 + j] = product[r0 : r0 + 32, 0:256]
-                    first[1, g, yy, xx * 2 + j] = product[r0 : r0 + 32, 256:512]
+                    for side in range(2):
+                        first[0, g, xx, yy * 2 + j, side] = product[r0 : r0 + 32, side * 128 : side * 128 + 128]
+                        first[1, g, yy, xx * 2 + j, side] = product[r0 : r0 + 32, side * 128 + 256 : side * 128 + 384]
             return carry
 
         lax.fori_loop(0, 4, block, 0)
@@ -340,28 +353,30 @@
 
     def middle(g):
         for part in range(2):
-            done = finish(0, part, g)
+            low, high = finish(0, part, g)
             for t in range(4):
-                second[part, g, t] = done[2 * t : 2 * t + 2].astype(WIRE)
+                half = (low, high)[t // 2].reshape(2, 2, 2, 32, 128)
+                second[part, g, t] = half[t % 2]
             begin(1, part, g)
 
     def last(g):
-        for part in range(2):
-            done = finish(1, part, g)
-            for j in range(2):
-                z_out[2 * g + j, part] = done[j].astype(WIRE)
+        parts = [finish(1, part, g) for part in range(2)]
         for j in range(2):
-            o = Z_ORDER[2 * g + j]
-            if o:
-                copy = remote(z_out.at[2 * g + j], z_in.at[o], z_send.at[o], z_recv.at[o], z_peers[o - 1])
-                copy.start()
-                pending.append(copy)
-
-    for tick in range(-1, NGROUPS + 4):
+            slot = 2 * g + j
+            value = jnp.concatenate([parts[0][j], parts[1][j]], axis=0)
+            o = Z_ORDER[slot]
+            if o == 0:
+                return value
+            encode(value, z_out.at[slot])
+            copy = remote(z_out.at[slot], z_in.at[o], z_send.at[o], z_recv.at[o], z_peers[o - 1])
+            copy.start()
+            pending.append(copy)
+
+    for tick in range(-1, NGROUPS + 3):
         if tick + 1 < NGROUPS:
             compute(tick + 1)
         if 0 <= tick - 3 < NGROUPS:
-            last(tick - 3)
+            sums = last(tick - 3)
         if 0 <= tick - 2 < NGROUPS:
             for part in range(2):
                 relay(1, part, tick - 2)
@@ -371,49 +386,48 @@
             for part in range(2):
                 relay(0, part, tick)
 
-    sums = z_out[Z_ORDER.index(0)].astype(F32)
     for o in (1, 7, 2, 6, 3, 5, 4):
         remote(z_out.at[0], z_in.at[o], z_send.at[o], z_recv.at[o], z_peers[o - 1]).wait_recv()
-        sums = sums + z_in[o].astype(F32)
-    total[...] = sums
+        sums = sums + decode(z_in.at[o])
+    encode(sums, ag_out)
     copies = []
-    for o in (4, 3, 5, 2, 6, 1, 7):
-        copy = remote(total, gathered.at[o], ag_send.at[o], ag_recv.at[o], ctx_peers[o - 1])
+    for o in FAR_FIRST:
+        copy = remote(ag_out, ag_in.at[o], ag_send.at[o], ag_recv.at[o], ctx_peers[o - 1])
         copy.start()
         copies.append(copy)
-    out_ref[ctx] = sums
+    out_ref[ctx] = decode(ag_out).reshape(4, 32, 128)
     for copy in pending:
         copy.wait_send()
     for copy in copies:
         copy.wait()
     for o in range(1, 8):
-        out_ref[lax.rem(ctx + 8 - o, 8)] = gathered[o]
+        out_ref[lax.rem(ctx + 8 - o, 8)] = decode(ag_in.at[o]).reshape(4, 32, 128)
 
 
 def reduce_gradient(dkv, hidden):
     rows = hidden.shape[0]
     dma = pltpu.SemaphoreType.DMA
-    unit = (32, 256)
+    codes = jnp.int16
     return pl.pallas_call(
         reduce_kernel,
-        out_shape=jax.ShapeDtypeStruct((8, 2, *unit), F32),
+        out_shape=jax.ShapeDtypeStruct((8, 4, 32, 128), F32),
         in_specs=[pl.BlockSpec(memory_space=pltpu.VMEM), pl.BlockSpec(memory_space=pl.ANY)],
         out_specs=pl.BlockSpec(memory_space=pltpu.VMEM),
         scratch_shapes=[
             pltpu.VMEM((16, 2 * rows, 512), BF16),
-            pltpu.VMEM((8, rows, 256), WIRE),
+            pltpu.VMEM((8, rows + 16, 256), codes),
             pltpu.VMEM((2 * rows, 256), BF16),
             pltpu.VMEM((256, 2 * rows), BF16),
-            pltpu.VMEM((2, NGROUPS, 4, 8, *unit), WIRE),
-            pltpu.VMEM((2, NGROUPS, 2, 4, *unit), WIRE),
-            pltpu.VMEM((2, NGROUPS, 2, 8, *unit), WIRE),
-            pltpu.VMEM((2, NGROUPS, 4, 2, *unit), WIRE),
-            pltpu.VMEM((2, NGROUPS, 2, 1, *unit), WIRE),
-            pltpu.VMEM((2, NGROUPS, 2, 2, *unit), WIRE),
-            pltpu.VMEM((8, 2, *unit), WIRE),
-            pltpu.VMEM((8, 2, *unit), WIRE),
-            pltpu.VMEM((2, *unit), F32),
-            pltpu.VMEM((8, 2, *unit), F32),
+            pltpu.VMEM((2, NGROUPS, 4, 8, 2, 32, 128), F32),
+            pltpu.VMEM((2, NGROUPS, 6, 272, 128), codes),
+            pltpu.VMEM((2, NGROUPS, 6, 272, 128), codes),
+            pltpu.VMEM((2, NGROUPS, 4, 2, 2, 32, 128), F32),
+            pltpu.VMEM((2, NGROUPS, 6, 80, 128), codes),
+            pltpu.VMEM((2, NGROUPS, 6, 80, 128), codes),
+            pltpu.VMEM((8, 144, 128), codes),
+            pltpu.VMEM((8, 144, 128), codes),
+            pltpu.VMEM((144, 128), codes),
+            pltpu.VMEM((8, 144, 128), codes),
             dma((16,)), dma((16,)), dma((16,)), dma((8,)), dma((8,)), dma, dma,
             dma((2, NGROUPS, 6)), dma((2, NGROUPS, 6)), dma((2, NGROUPS, 6)), dma((2, NGROUPS, 6)),
             dma((8,)), dma((8,)), dma((8,)), dma((8,)),
@@ -426,8 +440,8 @@
 
 
 def adam_kernel(grad_t, m_codes, m_scales, v_codes, v_scales, update, m_norm, m_absmax, v_norm, v_absmax, grad):
-    for part in range(2):
-        grad[pl.ds(part * 256, 256), :] = grad_t[:, part].reshape(256, 256).T
+    for q in range(4):
+        grad[pl.ds(q * 128, 128), :] = grad_t[:, q].reshape(256, 128).T
 
     def block(b, carry):
         rows = pl.ds(pl.multiple_of(b * 8, 8), 8)

time: 133 us -> 106 us (0.80)
  Pallas kernels: 126 us -> 99.4 us
    pallas_call x1, Pallas kernels: 92.6 us -> 65.6 us  [reduce_gradient(): pl.pallas_call(reduce_kernel, out_shape=jax.ShapeDtypeStruct((8, 4, 32, 1...]
where the time goes in v3:
time: 106 us
  Pallas kernels  99.4 us (94%)
  local copies, waits for them, and re-layouts  5.58 us (5%)
    pallas_call x1, Pallas kernels, reduce_gradient(): pl.pallas_call(reduce_kernel, out_shape=jax.ShapeDtypeStruct((8, 4, 32, 1...  65.6 us
    pallas_call x1, Pallas kernels, attention(): pl.pallas_call(attention_kernel, out_shape=[jax.ShapeDtypeStruct(queries....  15.7 us
    pallas_call x1, Pallas kernels, gather(): pl.pallas_call(gather_kernel, out_shape=[shape, shape], in_specs=[any_spa...  14.7 us
    unnamed x20, local copies, waits for them, and re-layouts  5.58 us
    pallas_call x1, Pallas kernels, adam(): pl.pallas_call(adam_kernel, out_shape=[big, big, small, big, small], in_s...  3.39 us

profile of v3, /device:TPU:8, one launch (start us, length us, event | category | flops | bytes accessed | tf_op | source)
XLA Modules:
  0.0 105.7 jit_solution(11059356283360919055)
XLA Ops:
  0.6 0.0 copy-start.7
  0.6 0.0 copy-start.6
  0.7 14.7 %gather_kv.1 = (bf16[1536,128]{1,0:T(8,128)(2,1)}, bf16[1536,128]{1,0:T(8,128)(2,1)}) custom-call(bf16[192,128]{1,0:T(8,128)(2,1)} %bitcast.9, bf16[192,128]{1,0:T(8,128)(2,1)} %bitcast.10), custom_call_target="tpu_custom_call" | custom-call | tf_op jit(solution)/shard_map/gather_kv/pallas_call | solution.py:84
  15.4 0.0 copy-start
  15.4 1.1 %copy-done = bf16[1,192,2048]{2,1,0:T(8,128)(2,1)S(1)} copy-done((bf16[1,192,2048]{2,1,0:T(8,128)(2,1)S(1)}, bf16[1,192,2048]{2,1,0:T(8,128)(2,1)}, u32[]{:S(2)}) %copy-start) | copy-done | bytes 786456
  16.5 0.0 copy-start.1
  16.5 1.1 %copy-done.1 = bf16[1,192,2048]{2,1,0:T(8,128)(2,1)S(1)} copy-done((bf16[1,192,2048]{2,1,0:T(8,128)(2,1)S(1)}, bf16[1,192,2048]{2,1,0:T(8,128)(2,1)}, u32[]{:S(2)}) %copy-start.1) | copy-done | bytes 786456
  17.7 0.0 copy-start.4
  17.7 1.0 copy-done.4
  18.7 0.0 copy-start.5
  18.7 1.0 copy-done.5
  19.6 0.0 copy-start.8
  19.7 0.7 copy-done.8
  20.3 0.0 copy-start.9
  20.3 0.7 copy-done.9
  21.0 0.0 copy-start.2
  21.0 0.0 copy-start.3
  21.0 15.7 %attention_backward.1 = (bf16[192,2048]{1,0:T(8,128)(2,1)}, s16[8,208,256]{2,1,0:T(8,128)(2,1)S(1)}) custom-call(s32[16]{0:T(128)S(1)} %copy-done.8, s32[1,8]{1,0:T(1,128)S(1)} %copy-done.9, bf16[192,2048]{1,0:T(8,128)(2,1)S(1)} %bitcast.6, bf16[192,2048]{1,0:T(8,128)(2,1)S(1)} %bitcast.7, bf16[1536,128]{1,0:T(8,128)(2,1)S(1)} %copy-done.4, ...), custom_call_target="tpu_custom_call" | custom-call | tf_op jit(solution)/shard_map/attention_backward/pallas_call | solution.py:199
  36.6 65.6 %project_and_reduce.1.grad_t = f32[8,4,32,128]{3,2,1,0:T(8,128)S(1)} custom-call(s16[8,208,256]{2,1,0:T(8,128)(2,1)S(1)} %get-tuple-element.18.dkv_ref, bf16[192,16384]{1,0:T(8,128)(2,1)} %bitcast.8), custom_call_target="tpu_custom_call" | custom-call | tf_op jit(solution)/shard_map/project_and_reduce/pallas_call | solution.py:411
  102.3 0.0 copy-done.7
  102.3 0.0 copy-done.6
  102.3 0.0 copy-done.2
  102.3 0.0 copy-done.3
  102.3 3.4 %adam.1 = (f32[512,256]{1,0:T(8,128)}, f32[512,256]{1,0:T(8,128)}, f32[64]{0:T(128)}, f32[512,256]{1,0:T(8,128)}, f32[64]{0:T(128)}) custom-call(f32[8,4,32,128]{3,2,1,0:T(8,128)S(1)} %project_and_reduce.1.grad_t, s32[512,256]{1,0:T(8,128)S(1)} %copy-done.2, f32[64]{0:T(128)S(1)} %copy-done.6, s32[512,256]{1,0:T(8,128)S(1)} %copy-done.3, f32[64]{0:T(128)S(1)} %copy-done.7), custom_call_target="tpu_custom_call" | custom-call | tf_op jit(solution)/shard_map/adam/pallas_call | solution.py:468
Async XLA Ops:
  0.6 101.6 %copy-start.7 = (f32[64]{0:T(128)S(1)}, f32[64]{0:T(128)}, u32[]{:S(2)}) copy-start(f32[64]{0:T(128)} %v_scales.1) | copy-start | bytes 772
  0.6 101.6 %copy-start.6 = (f32[64]{0:T(128)S(1)}, f32[64]{0:T(128)}, u32[]{:S(2)}) copy-start(f32[64]{0:T(128)} %m_scales.1) | copy-start | bytes 772
  15.4 1.1 %copy-start = (bf16[1,192,2048]{2,1,0:T(8,128)(2,1)S(1)}, bf16[1,192,2048]{2,1,0:T(8,128)(2,1)}, u32[]{:S(2)}) copy-start(bf16[1,192,2048]{2,1,0:T(8,128)(2,1)} %param.11) | copy-start | bytes 2359300
  16.5 1.1 %copy-start.1 = (bf16[1,192,2048]{2,1,0:T(8,128)(2,1)S(1)}, bf16[1,192,2048]{2,1,0:T(8,128)(2,1)}, u32[]{:S(2)}) copy-start(bf16[1,192,2048]{2,1,0:T(8,128)(2,1)} %param.14) | copy-start | bytes 2359300
  17.7 1.0 copy-start.4
  18.7 1.0 copy-start.5
  19.6 0.7 copy-start.8
  20.3 0.7 copy-start.9
  21.0 81.3 %copy-start.2 = (s32[512,256]{1,0:T(8,128)S(1)}, s32[512,256]{1,0:T(8,128)}, u32[]{:S(2)}) copy-start(s32[512,256]{1,0:T(8,128)} %m_codes.1) | copy-start | bytes 1572868
  21.0 81.3 %copy-start.3 = (s32[512,256]{1,0:T(8,128)S(1)}, s32[512,256]{1,0:T(8,128)}, u32[]{:S(2)}) copy-start(s32[512,256]{1,0:T(8,128)} %v_codes.1) | copy-start | bytes 1572868

commit v4 on v0

v4 whole, which is shorter than its diff:
```python
import functools
import math

import jax
import jax.numpy as jnp
from jax import lax
from jax.experimental import pallas as pl
from jax.experimental.pallas import tpu as pltpu
from jax.sharding import PartitionSpec as P

STEP = 10
SPAN = 96
WINDOW = 7
HEAD = 128
GROUP = 8
NGROUPS = 2
FAR_FIRST = (4, 3, 5, 2, 6, 1, 7)
DISTANCES = ((4, 2), (0, 6))
F32 = jnp.float32
BF16 = jnp.bfloat16
MESH = pl.DeviceIdType.MESH


def remote(src, dst, send, recv, device):
    return pltpu.make_async_remote_copy(
        src_ref=src, dst_ref=dst, send_sem=send, recv_sem=recv, device_id=device, device_id_type=MESH
    )


def greet(devices):
    barrier = pltpu.get_barrier_semaphore()
    for device in devices:
        pl.semaphore_signal(barrier, inc=1, device_id=device, device_id_type=MESH)
    pl.semaphore_wait(barrier, len(devices))


def encode(values, message):
    rows = values.shape[0]
    top = jnp.max(jnp.abs(values), axis=0, keepdims=True)
    power = jnp.ceil(jnp.log2(jnp.maximum(top, 1e-30)))
    codes = jnp.round(values * (jnp.exp2(-power) * 32000.0))
    message[pl.ds(0, rows), :] = codes.astype(jnp.int32).astype(jnp.int16)
    head = jnp.broadcast_to(power, (16, values.shape[1]))
    message[pl.ds(rows, 16), :] = head.astype(jnp.int32).astype(jnp.int16)


def decode(message):
    rows = message.shape[0] - 16
    power = message[pl.ds(rows, 16), :].astype(jnp.int32).astype(F32)[0:1, :]
    codes = message[pl.ds(0, rows), :].astype(jnp.int32).astype(F32)
    return codes * (jnp.exp2(power) * (1.0 / 32000.0))


def dot_t(left, right):
    return lax.dot_general(left, right, (((1,), (1,)), ((), ())), preferred_element_type=F32)


def window_of(order, place, stored, window):
    def pick(r, carry):
        wanted = place - (WINDOW - 1) + r
        block = jnp.zeros((SPAN, HEAD), BF16)
        for s in range(16):
            weight = jnp.where(order[s] == wanted, 1.0, 0.0).astype(BF16)
            block = block + stored[pl.ds(s * SPAN, SPAN), :] * weight
        window[pl.ds(pl.multiple_of(r * SPAN, SPAN), SPAN), :] = block
        return carry

    lax.fori_loop(0, WINDOW, pick, 0)


def mask_bias(place, lens, bias):
    width = GROUP * SPAN
    lane = lax.broadcasted_iota(jnp.int32, (1, width), 1)
    head = jnp.zeros_like(lane)
    for h in range(1, GROUP):
        head = head + (lane >= h * SPAN).astype(jnp.int32)
    query_pos = place * SPAN + lane - head * SPAN
    begin = jnp.zeros_like(lane)
    end = jnp.int32(0)
    for k in range(8):
        end = end + lens[0, k]
        begin = jnp.where(query_pos >= end, end, begin)
    for r in range(WINDOW):
        key_pos = (place - (WINDOW - 1) + r) * SPAN + lax.broadcasted_iota(jnp.int32, (SPAN, width), 0)
        allowed = (key_pos <= query_pos) & (key_pos >= begin)
        bias[pl.ds(r * SPAN, SPAN), :] = jnp.where(allowed, 0.0, -1e30)


def heads_of(ref, qb, grp):
    rows = pl.ds(pl.multiple_of(qb * SPAN, SPAN), SPAN)
    wide = GROUP * HEAD
    lanes = [pl.ds(pl.multiple_of(grp * wide, wide) + h * HEAD, HEAD) for h in range(GROUP)]
    return rows, lanes, jnp.concatenate([ref[rows, c] for c in lanes], axis=0)


def softmax_numerators(k7, queries, bias, expo_scr, inv_scr):
    factor = math.log2(math.e) / math.sqrt(HEAD)
    width = GROUP * SPAN
    parts = [pl.ds(r * SPAN, SPAN) for r in range(WINDOW)]
    expo_scr[...] = dot_t(k7[...], queries)
    top = jnp.full((8, width), -3e38, F32)
    for part in parts:
        scores = expo_scr[part, :] + bias[part, :]
        expo_scr[part, :] = scores
        top = jnp.maximum(top, jnp.max(scores.reshape(SPAN // 8, 8, width), axis=0))
    top = jnp.max(top, axis=0, keepdims=True)
    denom = jnp.zeros((8, width), F32)
    for part in parts:
        expo = jnp.exp2((expo_scr[part, :] - top) * factor)
        expo_scr[part, :] = expo
        denom = denom + jnp.sum(expo.reshape(SPAN // 8, 8, width), axis=0)
    inv_scr[...] = jnp.broadcast_to(1.0 / jnp.sum(denom, axis=0, keepdims=True), (8, width))


def softmax_terms(v7, cots, expo_scr, inv_scr, d_scr, p_scr, ds_scr):
    width = GROUP * SPAN
    parts = [pl.ds(r * SPAN, SPAN) for r in range(WINDOW)]
    d_scr[...] = dot_t(v7[...], cots)
    inv = inv_scr[0:1, :]
    weighted = jnp.zeros((8, width), F32)
    for part in parts:
        prob = expo_scr[part, :] * inv
        expo_scr[part, :] = prob
        p_scr[part, :] = prob.astype(BF16)
        weighted = weighted + jnp.sum((prob * d_scr[part, :]).reshape(SPAN // 8, 8, width), axis=0)
    delta = jnp.sum(weighted, axis=0, keepdims=True)
    for part in parts:
        ds_scr[part, :] = (expo_scr[part, :] * (d_scr[part, :] - delta)).astype(BF16)


def messages(order, places, found, out, gain):
    def write(c, carry):
        halves = []
        for half in range(2):
            place = order[2 * c + half]
            value = jnp.zeros((SPAN, HEAD), F32)
            for qb in range(2):
                for r in range(WINDOW):
                    weight = jnp.where(place - (places[qb] - (WINDOW - 1)) == r, 1.0, 0.0)
                    value = value + found[qb, pl.ds(r * SPAN, SPAN), :] * weight
            halves.append(value)
        encode(jnp.concatenate(halves, axis=0) * gain, out.at[c])
        return carry

    lax.fori_loop(0, 8, write, 0)


def backward_kernel(
    order, lens, q_hbm, g_hbm, k_hbm, v_hbm, hid, dq_hbm, out_ref,
    q_ref, g_ref, kall, vall, k7, v7, k7t, bias, expo_all, inv_all, d_scr, p_scr, ds_all, dkw, dvw, dk_out, dv_out, dk_in, dv_in, dq_ref,
    load_sem, kv_send, kv_recv, dk_send, dk_recv, dv_send, dv_recv,
    held, dkv2, dkvt, first, out1, in1, second, out2, in2, z_out, z_in, total, ag_out, ag_in,
    hid_own, hid_send, hid_recv, near_send, near_recv, pair_send, pair_recv,
    send1, recv1, send2, recv2, z_send, z_recv, ag_send, ag_recv,
):
    dp, ctx = lax.axis_index("dp"), lax.axis_index("ctx")
    x, ylo = ctx // 2, lax.rem(ctx, 2)
    z, yhi, core = dp // 4, lax.rem(dp // 2, 2), lax.rem(dp, 2)
    y = yhi * 2 + ylo
    rows = hid.shape[0]

    def at(xx, yy, zz):
        return (zz * 4 + (yy // 2) * 2 + core, xx * 2 + lax.rem(yy, 2))

    x_ring = (x, *[at(lax.rem(x + k, 4), y, z) for k in range(1, 4)])
    y_ring = (y, *[at(x, lax.rem(y + k, 4), z) for k in range(1, 4)])
    pair = (dp + 1 - 2 * core, ctx)
    ctx_peers = [(dp, lax.rem(ctx + o, 8)) for o in range(1, 8)]
    even_peers = [at(x, y, lax.rem(z + o, 8)) for o in (2, 4, 6)]
    y_far = at(x, lax.rem(y + 2, 4), z)
    across = at(x, lax.rem(y + 3 + 2 * ylo, 4), z)

    def columns(zz, kind, j, yh, c):
        distance = 4 - 4 * j + kind * (8 * j - 2)
        block = lax.rem(zz + distance, 8) * 4 + yh * 2 + c
        return pl.ds(pl.multiple_of(block * 512, 512), 512)

    parity = lax.rem(z, 2)
    wanted = lax.rem(z, 4) // 2
    near = []
    for n in range(2):
        zz = lax.rem(z + (1 - 2 * n) * (1 - 2 * parity) + 8, 8)
        for c in range(2):
            near.append((zz, lax.rem(core + c, 2)))
    sharers = [(zz * 4 + yhi * 2 + cc, ctx) for zz, cc in near]

    mine = pl.ds(pl.multiple_of(ctx * rows, rows), rows)
    loads = [
        pltpu.make_async_copy(src, dst, load_sem.at[k])
        for k, (src, dst) in enumerate(
            ((k_hbm, kall.at[mine]), (v_hbm, vall.at[mine]), (q_hbm, q_ref), (g_hbm, g_ref))
        )
    ]
    for copy in loads:
        copy.start()
    greet([*ctx_peers, *even_peers, *sharers, pair, across, y_far])
    kv_copies = []
    for which, (src, dst) in enumerate(((k_hbm, kall), (v_hbm, vall))):
        for o in FAR_FIRST:
            copy = remote(src, dst.at[mine], kv_send.at[which, o], kv_recv.at[which, o], ctx_peers[o - 1])
            copy.start()
            kv_copies.append(copy)
    near_copies = []
    for j in range(2):
        for yh in range(2):
            for n, (zz, cc) in enumerate(near):
                slot, block = j * 4 + wanted * 2 + yh, 2 + n % 2
                copy = remote(
                    hid.at[:, columns(zz, wanted, j, yh, cc)],
                    held.at[slot, pl.ds(block * rows, rows)],
                    near_send.at[j * 2 + yh, n],
                    near_recv.at[slot, n % 2],
                    sharers[n],
                )
                copy.start()
                near_copies.append(copy)
    own, swaps = [], []
    for slot in range(8):
        j, kind, yh = slot // 4, slot // 2 % 2, slot % 2
        own.append(
            pltpu.make_async_copy(
                hid.at[:, columns(z, kind, j, yh, core)], held.at[slot, pl.ds(0, rows)], hid_own.at[slot]
            )
        )
        own[slot].start()
        copy = remote(
            hid.at[:, columns(z, kind, j, yh, 1 - core)],
            held.at[slot, pl.ds(rows, rows)],
            hid_send.at[slot],
            hid_recv.at[slot],
            pair,
        )
        copy.start()
        swaps.append(copy)

    places = [order[2 * ctx], order[2 * ctx + 1]]
    for qb in range(2):
        mask_bias(places[qb], lens, bias.at[qb])
    dvw[...] = jnp.zeros_like(dvw)
    dkw[...] = jnp.zeros_like(dkw)
    def all_here(which, src, dst):
        loads[which].wait()
        for o in FAR_FIRST:
            theirs = pl.ds(pl.multiple_of(lax.rem(ctx + 8 - o, 8) * rows, rows), rows)
            remote(src, dst.at[theirs], kv_send.at[which, o], kv_recv.at[which, o], ctx_peers[o - 1]).wait_recv()

    reach = pl.ds(0, WINDOW * SPAN)
    steps = 2 * 16 // GROUP
    scale = 1.0 / math.sqrt(HEAD)
    all_here(0, k_hbm, kall)
    loads[2].wait()
    for qb in range(2):
        window_of(order, places[qb], kall, k7.at[qb])

    def numerator_step(it, carry):
        qb, grp = it // (steps // 2), lax.rem(it, steps // 2)
        queries = heads_of(q_ref, qb, grp)[2]
        softmax_numerators(k7.at[qb], queries, bias.at[qb], expo_all.at[it], inv_all.at[it])
        return carry

    lax.fori_loop(0, steps, numerator_step, 0)
    all_here(1, v_hbm, vall)
    loads[3].wait()
    for qb in range(2):
        window_of(order, places[qb], vall, v7.at[qb])

    def score_step(it, carry):
        qb, grp = it // (steps // 2), lax.rem(it, steps // 2)
        cots = heads_of(g_ref, qb, grp)[2]
        softmax_terms(v7.at[qb], cots, expo_all.at[it], inv_all.at[it], d_scr, p_scr, ds_all.at[it])
        dvw[qb, reach, :] += jnp.dot(p_scr[...], cots, preferred_element_type=F32)
        return carry

    lax.fori_loop(0, steps, score_step, 0)

    def exchange(out, into, send, recv):
        copies = []
        for o in FAR_FIRST:
            copy = remote(out.at[lax.rem(ctx + o, 8)], into.at[o], send.at[o], recv.at[o], ctx_peers[o - 1])
            copy.start()
            copies.append(copy)
        return copies

    messages(order, places, dvw, dv_out, 1.0)
    dv_copies = exchange(dv_out, dv_in, dv_send, dv_recv)

    def key_step(it, carry):
        qb, grp = it // (steps // 2), lax.rem(it, steps // 2)
        queries = heads_of(q_ref, qb, grp)[2]
        dkw[qb, reach, :] += jnp.dot(ds_all[it], queries, preferred_element_type=F32)
        return carry

    lax.fori_loop(0, steps, key_step, 0)
    messages(order, places, dkw, dk_out, scale)
    dk_copies = exchange(dk_out, dk_in, dk_send, dk_recv)

    for qb in range(2):
        k7t[qb] = k7[qb].astype(F32).T.astype(BF16)

    def query_step(it, carry):
        qb, grp = it // (steps // 2), lax.rem(it, steps // 2)
        query_rows, lanes, _ = heads_of(q_ref, qb, grp)
        dq = (jnp.dot(k7t[qb], ds_all[it], preferred_element_type=F32) * scale).T.astype(BF16)
        for h in range(GROUP):
            dq_ref[query_rows, lanes[h]] = dq[h * SPAN : (h + 1) * SPAN, :]
        return carry

    lax.fori_loop(0, steps, query_step, 0)
    dq_copy = pltpu.make_async_copy(dq_ref, dq_hbm, load_sem.at[4])
    dq_copy.start()

    dkv_copies = []
    for side, (copies, out, into) in enumerate(((dk_copies, dk_out, dk_in), (dv_copies, dv_out, dv_in))[::-1]):
        for copy in copies:
            copy.wait()
        value = decode(out.at[ctx])
        for o in range(1, 8):
            value = value + decode(into.at[o])
        lanes = pl.ds((1 - side) * HEAD, HEAD)
        dkv2[pl.ds(0, rows), lanes] = value.astype(BF16)
        for n, device in enumerate([pair, *sharers]):
            start, arrival = rows, 0
            if n:
                arrival = 1 + 2 * wanted + (n - 1) % 2
                start = (1 + arrival) * rows
            copy = remote(
                dkv2.at[pl.ds(0, rows), lanes],
                dkv2.at[pl.ds(pl.multiple_of(start, rows), rows), lanes],
                pair_send.at[side, n],
                pair_recv.at[side, arrival],
                device,
            )
            copy.start()
            dkv_copies.append(copy)
    for side in range(2):
        for n in range(5):
            lanes = pl.ds((1 - side) * HEAD, HEAD)
            remote(
                dkv2.at[pl.ds(0, rows), lanes],
                dkv2.at[pl.ds((1 + n) * rows, rows), lanes],
                pair_send.at[side, n],
                pair_recv.at[side, n],
                pair,
            ).wait_recv()
    dkvt[...] = dkv2[...].astype(F32).T.astype(BF16)

    rings = ((x_ring, y_ring), (y_ring, x_ring))
    pending = []

    def flat(value):
        return value.reshape(-1, 128)

    def piece(part, g, place, high):
        return flat(first[part, g, place, pl.ds(4 * high, 4)])

    def copy_of(part, g, k):
        device = rings[part][0][1 if k % 2 == 0 else 3]
        return remote(out1.at[part, g, k], in1.at[part, g, k], send1.at[part, g, k], recv1.at[part, g, k], device)

    def post(part, g, k, value):
        encode(value, out1.at[part, g, k])
        copy = copy_of(part, g, k)
        copy.start()
        pending.append(copy)

    def arrived(part, g, k):
        copy_of(part, g, k).wait_recv()
        return decode(in1.at[part, g, k])

    def begin(part, g):
        place = rings[part][0][0]
        after, before, opposite = lax.rem(place + 1, 4), lax.rem(place + 3, 4), lax.rem(place + 2, 4)
        for k, (owner, high) in enumerate(((opposite, 0), (opposite, 1), (after, 1), (before, 0))):
            post(part, g, k, piece(part, g, owner, high))

    def relay(part, g):
        place = rings[part][0][0]
        after, before = lax.rem(place + 1, 4), lax.rem(place + 3, 4)
        for k, (owner, high) in enumerate(((after, 0), (before, 1))):
            post(part, g, 4 + k, arrived(part, g, k) + piece(part, g, owner, high))

    def finish(part, g):
        place = rings[part][0][0]
        low = arrived(part, g, 3) + arrived(part, g, 4) + piece(part, g, place, 0)
        high = arrived(part, g, 2) + arrived(part, g, 5) + piece(part, g, place, 1)
        return low, high

    def direct(part, g, k):
        return remote(
            out2.at[part, g, k], in2.at[part, g, k], send2.at[part, g, k], recv2.at[part, g, k], rings[part][1][k]
        )

    def compute(g):
        for slot in range(4 * g, 4 * g + 4):
            own[slot].wait()
            swaps[slot].wait()
            for c in range(2):
                block = pl.ds((2 + c) * rows, rows)
                remote(
                    hid.at[:, pl.ds(0, 512)], held.at[slot, block], near_send.at[0, 0], near_recv.at[slot, c], pair
                ).wait_recv()

        def block(k, carry):
            kind, yh = k // 2, lax.rem(k, 2)
            theirs = pl.ds(pl.multiple_of(2 * rows * (1 + kind), 128), 2 * rows)
            here, both = pl.ds(0, 2 * rows), pl.ds(2 * rows, 2 * rows)
            product = jnp.dot(dkvt[:, 0 : 2 * rows], held[4 * g + k, here], preferred_element_type=F32)
            product = product + jnp.dot(
                dkvt[:, theirs], held[4 * g + k, both], preferred_element_type=F32
            )
            for xx in range(4):
                for yl in range(2):
                    r0 = (xx * 2 + yl) * 32
                    yy = yh * 2 + yl
                    for side in range(2):
                        first[0, g, xx, yy * 2 + kind, side] = product[r0 : r0 + 32, side * 128 : side * 128 + 128]
                        first[1, g, yy, xx * 2 + kind, side] = product[r0 : r0 + 32, side * 128 + 256 : side * 128 + 384]
            return carry

        lax.fori_loop(0, 4, block, 0)
        for part in range(2):
            begin(part, g)

    def middle(g):
        for part in range(2):
            low, high = finish(part, g)
            for t in range(4):
                half = (low, high)[t // 2].reshape(2, 2, 2, 32, 128)
                second[part, g, t] = half[t % 2]
            place = rings[part][1][0]
            for k in (2, 1, 3):
                encode(flat(second[part, g, lax.rem(place + k, 4)]), out2.at[part, g, k])
                copy = direct(part, g, k)
                copy.start()
                pending.append(copy)

    def last(g):
        parts = []
        for part in range(2):
            value = flat(second[part, g, rings[part][1][0]])
            for k in (1, 3, 2):
                direct(part, g, k).wait_recv()
                value = value + decode(in2.at[part, g, k])
            parts.append(value.reshape(2, 64, 128))
        for kind in range(2):
            slot = 2 * g + kind
            value = jnp.concatenate([parts[0][kind], parts[1][kind]], axis=0)
            o = DISTANCES[g][kind]
            if o == 0:
                total[...] = value
                continue
            encode(value, z_out.at[slot])
            copy = remote(z_out.at[slot], z_in.at[o], z_send.at[o], z_recv.at[o], even_peers[o // 2 - 1])
            copy.start()
            pending.append(copy)

    compute(0)
    for part in range(2):
        relay(part, 0)
    compute(1)
    middle(0)
    for part in range(2):
        relay(part, 1)
    last(0)
    middle(1)
    last(1)

    sums = total[...]
    for o in (4, 2, 6):
        remote(z_out.at[0], z_in.at[o], z_send.at[o], z_recv.at[o], even_peers[o // 2 - 1]).wait_recv()
        sums = sums + decode(z_in.at[o])
    encode(sums, ag_out)
    copies = []
    for o in FAR_FIRST:
        copy = remote(ag_out, ag_in.at[o], ag_send.at[o], ag_recv.at[o], ctx_peers[o - 1])
        copy.start()
        copies.append(copy)
    out_ref[ctx] = decode(ag_out).reshape(4, 32, 128)
    for copy in pending:
        copy.wait_send()
    for copy in [*kv_copies, *near_copies, *dkv_copies]:
        copy.wait_send()
    dq_copy.wait()
    for copy in copies:
        copy.wait()
    for o in range(1, 8):
        out_ref[lax.rem(ctx + 8 - o, 8)] = decode(ag_in.at[o]).reshape(4, 32, 128)


def backward(order, lens, queries, cots, keys, values, hidden):
    rows = hidden.shape[0]
    dma = pltpu.SemaphoreType.DMA
    codes = jnp.int16
    reach, width = WINDOW * SPAN, GROUP * SPAN
    hbm = pl.BlockSpec(memory_space=pl.ANY)
    smem = pl.BlockSpec(memory_space=pltpu.SMEM)
    return pl.pallas_call(
        backward_kernel,
        out_shape=[
            jax.ShapeDtypeStruct(queries.shape, BF16),
            jax.ShapeDtypeStruct((8, 4, 32, 128), F32),
        ],
        in_specs=[smem, smem, hbm, hbm, hbm, hbm, hbm],
        out_specs=[hbm, pl.BlockSpec(memory_space=pltpu.VMEM)],
        scratch_shapes=[
            pltpu.VMEM(queries.shape, BF16),
            pltpu.VMEM(queries.shape, BF16),
            pltpu.VMEM((8 * rows, HEAD), BF16),
            pltpu.VMEM((8 * rows, HEAD), BF16),
            pltpu.VMEM((2, reach, HEAD), BF16),
            pltpu.VMEM((2, reach, HEAD), BF16),
            pltpu.VMEM((2, HEAD, reach), BF16),
            pltpu.VMEM((2, reach, width), F32),
            pltpu.VMEM((32 // GROUP, reach, width), F32),
            pltpu.VMEM((32 // GROUP, 8, width), F32),
            pltpu.VMEM((reach, width), F32),
            pltpu.VMEM((reach, width), BF16),
            pltpu.VMEM((32 // GROUP, reach, width), BF16),
            pltpu.VMEM((2, reach, HEAD), F32),
            pltpu.VMEM((2, reach, HEAD), F32),
            pltpu.VMEM((8, rows + 16, HEAD), codes),
            pltpu.VMEM((8, rows + 16, HEAD), codes),
            pltpu.VMEM((8, rows + 16, HEAD), codes),
            pltpu.VMEM((8, rows + 16, HEAD), codes),
            pltpu.VMEM(queries.shape, BF16),
            dma((5,)), dma((2, 8)), dma((2, 8)), dma((8,)), dma((8,)), dma((8,)), dma((8,)),
            pltpu.VMEM((8, 4 * rows, 512), BF16),
            pltpu.VMEM((6 * rows, 256), BF16),
            pltpu.VMEM((256, 6 * rows), BF16),
            pltpu.VMEM((2, NGROUPS, 4, 8, 2, 32, 128), F32),
            pltpu.VMEM((2, NGROUPS, 6, 272, 128), codes),
            pltpu.VMEM((2, NGROUPS, 6, 272, 128), codes),
            pltpu.VMEM((2, NGROUPS, 4, 2, 2, 32, 128), F32),
            pltpu.VMEM((2, NGROUPS, 4, 144, 128), codes),
            pltpu.VMEM((2, NGROUPS, 4, 144, 128), codes),
            pltpu.VMEM((8, 144, 128), codes),
            pltpu.VMEM((8, 144, 128), codes),
            pltpu.VMEM((128, 128), F32),
            pltpu.VMEM((144, 128), codes),
            pltpu.VMEM((8, 144, 128), codes),
            dma((8,)), dma((8,)), dma((8,)), dma((4, 4)), dma((8, 2)), dma((2, 5)), dma((2, 5)),
            dma((2, NGROUPS, 6)), dma((2, NGROUPS, 6)), dma((2, NGROUPS, 4)), dma((2, NGROUPS, 4)),
            dma((8,)), dma((8,)), dma((8,)), dma((8,)),
        ],
        compiler_params=pltpu.CompilerParams(
            collective_id=0, has_side_effects=True, vmem_limit_bytes=60 * 2**20
        ),
        name="backward",
    )(order, lens, queries, cots, keys, values, hidden)


def adam_kernel(
    dq_in, grad_t, m_codes, m_scales, v_codes, v_scales, dq, update, m_norm, m_absmax, v_norm, v_absmax, grad
):
    dq[...] = dq_in[...]
    grad[...] = grad_t[:, 0].reshape(256, 128).T
    base = pl.program_id(0) * 16
    for b in range(16):
        rows = pl.ds(b * 8, 8)
        g = grad[rows, :]
        m = 0.9 * (m_codes[rows, :].astype(F32) * (m_scales[base + b] * (1.0 / 127.0))) + 0.1 * g
        v = 0.95 * (v_codes[rows, :].astype(F32) * (v_scales[base + b] * (1.0 / 255.0))) + 0.05 * g * g
        update[rows, :] = m * (1.0 / (1.0 - 0.9**STEP)) / (jnp.sqrt(v * (1.0 / (1.0 - 0.95**STEP))) + 1e-08)
        m_top = jnp.max(jnp.abs(m))
        v_top = jnp.max(v)
        m_absmax[base + b] = m_top
        v_absmax[base + b] = v_top
        m_norm[rows, :] = m / (m_top + 1e-06)
        v_norm[rows, :] = v / (v_top + 1e-06)


def adam(dq, grad_t, m_codes, m_scales, v_codes, v_scales):
    smem = pl.BlockSpec(memory_space=pltpu.SMEM)
    rows = pl.BlockSpec((128, 256), lambda q: (q, 0))
    slab = pl.BlockSpec((dq.shape[0] // 4, dq.shape[1]), lambda q: (q, 0))
    big = jax.ShapeDtypeStruct(m_codes.shape, F32)
    small = jax.ShapeDtypeStruct(m_scales.shape, F32)
    return pl.pallas_call(
        adam_kernel,
        grid=(4,),
        out_shape=[jax.ShapeDtypeStruct(dq.shape, dq.dtype), big, big, small, big, small],
        in_specs=[slab, pl.BlockSpec((8, 1, 32, 128), lambda q: (0, q, 0, 0)), rows, smem, rows, smem],
        out_specs=[slab, rows, rows, smem, rows, smem],
        scratch_shapes=[pltpu.VMEM((128, 256), F32)],
        compiler_params=pltpu.CompilerParams(vmem_limit_bytes=60 * 2**20),
        name="adam",
    )(dq, grad_t, m_codes, m_scales, v_codes, v_scales)


def shards(
    q_heads, keys, values, out_grad, hidden_in, doc_lengths, span_order, m_codes, m_scales, v_codes, v_scales
):
    dq, grad_t = backward(
        span_order, doc_lengths, q_heads[0], out_grad[0], keys[0], values[0], hidden_in[0]
    )
    dq, update, m_norm, m_absmax, v_norm, v_absmax = adam(dq, grad_t, m_codes, m_scales, v_codes, v_scales)
    return (dq[None], update, m_norm, m_absmax, v_norm, v_absmax)


def solution(mesh):
    in_specs = (
        P("dp", "ctx", None),
        P("dp", "ctx", None),
        P("dp", "ctx", None),
        P("dp", "ctx", None),
        P("dp", "ctx", None),
        P("dp", None),
        P(),
        P("dp", None),
        P("dp"),
        P("dp", None),
        P("dp"),
    )
    out_specs = (
        P("dp", "ctx", None),
        P("dp", None),
        P("dp", None),
        P("dp"),
        P("dp", None),
        P("dp"),
    )
    return jax.shard_map(shards, mesh=mesh, in_specs=in_specs, out_specs=out_specs, check_vma=False)
```

time: 550 us -> 88.3 us (0.16)
  waiting for transfers between devices: 345 us -> 0 us
  Pallas kernels: 0 us -> 87.1 us
  matrix products: 76.2 us -> 0 us
  blocking collectives: 60 us -> 0 us
  local copies, waits for them, and re-layouts: 33.6 us -> 0 us
  other arithmetic: 17.2 us -> 0 us
  between operations: 14 us -> 0.64 us
    reduce_scatter x2 -> x0, waiting for transfers between devices: 268 us -> none  [the longest x1 220 us: shards(): lax.psum_scatter(contract_rows(layer_in, own_low), 'dp', scatter_dimensio...]
    pallas_call x0 -> x2, Pallas kernels: none -> 87.1 us  [the longest x1 82.8 us: backward(): pl.pallas_call(backward_kernel, out_shape=[jax.ShapeDtypeStruct(queries.s...]
    psum x1 -> x0, waiting for transfers between devices: 77.3 us -> none  [shards(): grad = lax.psum(grad, 'ctx')]
    dot_general x22 -> x0, matrix products: 76.2 us -> none  [the longest x12 41.6 us: contract_cols(): lax.dot_general(left, right, (((1,), (1,)), ((), ())), preferred_element_...]
    all_gather x2 -> x0, blocking collectives: 60 us -> none  [the longest x1 30.8 us: shards(): lax.all_gather(values[0], 'ctx', axis=0, tiled=True)]
    reshape x7 -> x0, local copies, waits for them, and re-layouts: 10.7 us -> none  [the longest x6 10.1 us: block_masks(): jnp.broadcast_to(small[:, None, :], (rows, nheads, width))]
    reduce_sum x5 -> x0, other arithmetic: 5.83 us -> none  [the longest x3 4.94 us: forward_terms(): jnp.sum(expo, axis=1, keepdims=True)]
  transfers between devices with their start and end apart: 3 -> 0, of which waited for: 3 -> 0; matrix products, arithmetic and copies ran while one was open for 0% -> 0% of each run, Pallas kernels for 0% -> 0%
where the time goes in v4:
time: 88.3 us; the launch traced here: 87.8 us
  Pallas kernels  87.1 us (99%)
    pallas_call x1, Pallas kernels, backward(): pl.pallas_call(backward_kernel, out_shape=[jax.ShapeDtypeStruct(queries.s...  82.8 us
    pallas_call x1, Pallas kernels, adam(): pl.pallas_call(adam_kernel, grid=(4,), out_shape=[jax.ShapeDtypeStruct(dq...  4.34 us

profile of v4, /device:TPU:8, one launch (start us, length us, event | category | flops | bytes accessed | tf_op | source)
XLA Modules:
  0.0 87.8 jit_solution(12351997163507683973)
XLA Ops:
  0.6 82.8 %backward.1 = (bf16[192,2048]{1,0:T(8,128)(2,1)}, f32[8,4,32,128]{3,2,1,0:T(8,128)}) custom-call(s32[16]{0:T(128)} %order.1, s32[1,8]{1,0:T(1,128)} %lens.1, bf16[192,2048]{1,0:T(8,128)(2,1)} %bitcast.7, bf16[192,2048]{1,0:T(8,128)(2,1)} %bitcast.8, bf16[192,128]{1,0:T(8,128)(2,1)} %bitcast.9, bf16[192,128]{1,0:T(8,128)(2,1)} %bitcast.10, ...), custom_call_target="tpu_custom_call" | custom-call | tf_op jit(solution)/shard_map/backward/pallas_call | solution.py:497
  83.5 4.3 %adam.1 = (bf16[192,2048]{1,0:T(8,128)(2,1)}, f32[512,256]{1,0:T(8,128)}, f32[512,256]{1,0:T(8,128)}, f32[64]{0:T(128)}, f32[512,256]{1,0:T(8,128)}, /*index=5*/f32[64]{0:T(128)}) custom-call(bf16[192,2048]{1,0:T(8,128)(2,1)} %get-tuple-element.14.dq_in, f32[8,4,32,128]{3,2,1,0:T(8,128)} %get-tuple-element.15.grad_t, s32[512,256]{1,0:T(8,128)} %m_codes.1, ...), custom_call_target="tpu_custom_call" | custom-call | tf_op jit(solution)/shard_map/adam/pallas_call | solution.py:578

commit v5 on v4

--- a/solution.py
+++ b/solution.py
@@ -13,6 +13,7 @@
 WINDOW = 7
 HEAD = 128
 GROUP = 8
+EARLY = 12
 NGROUPS = 2
 FAR_FIRST = (4, 3, 5, 2, 6, 1, 7)
 DISTANCES = ((4, 2), (0, 6))
@@ -212,8 +213,9 @@
                     near_recv.at[slot, n % 2],
                     sharers[n],
                 )
-                copy.start()
                 near_copies.append(copy)
+                if len(near_copies) <= EARLY:
+                    copy.start()
     own, swaps = [], []
     for slot in range(8):
         j, kind, yh = slot // 4, slot // 2 % 2, slot % 2
@@ -332,6 +334,8 @@
             )
             copy.start()
             dkv_copies.append(copy)
+    for copy in near_copies[EARLY:]:
+        copy.start()
     for side in range(2):
         for n in range(5):
             lanes = pl.ds((1 - side) * HEAD, HEAD)

time: 88.3 us -> 82.3 us (0.932)
  Pallas kernels: 87.1 us -> 81.5 us
    pallas_call x1, Pallas kernels: 82.8 us -> 77.2 us  [backward(): pl.pallas_call(backward_kernel, out_shape=[jax.ShapeDtypeStruct(queries.s...]
where the time goes in v5:
time: 82.3 us; the launch traced here: 82.1 us
  Pallas kernels  81.5 us (99%)
    pallas_call x1, Pallas kernels, backward(): pl.pallas_call(backward_kernel, out_shape=[jax.ShapeDtypeStruct(queries.s...  77.2 us
    pallas_call x1, Pallas kernels, adam(): pl.pallas_call(adam_kernel, grid=(4,), out_shape=[jax.ShapeDtypeStruct(dq...  4.34 us

profile of v5, /device:TPU:8, one launch (start us, length us, event | category | flops | bytes accessed | tf_op | source)
XLA Modules:
  0.0 82.1 jit_solution(17238157975420417817)
XLA Ops:
  0.6 77.2 %backward.1 = (bf16[192,2048]{1,0:T(8,128)(2,1)}, f32[8,4,32,128]{3,2,1,0:T(8,128)}) custom-call(s32[16]{0:T(128)} %order.1, s32[1,8]{1,0:T(1,128)} %lens.1, bf16[192,2048]{1,0:T(8,128)(2,1)} %bitcast.7, bf16[192,2048]{1,0:T(8,128)(2,1)} %bitcast.8, bf16[192,128]{1,0:T(8,128)(2,1)} %bitcast.9, bf16[192,128]{1,0:T(8,128)(2,1)} %bitcast.10, ...), custom_call_target="tpu_custom_call" | custom-call | tf_op jit(solution)/shard_map/backward/pallas_call | solution.py:501
  77.8 4.3 %adam.1 = (bf16[192,2048]{1,0:T(8,128)(2,1)}, f32[512,256]{1,0:T(8,128)}, f32[512,256]{1,0:T(8,128)}, f32[64]{0:T(128)}, f32[512,256]{1,0:T(8,128)}, /*index=5*/f32[64]{0:T(128)}) custom-call(bf16[192,2048]{1,0:T(8,128)(2,1)} %get-tuple-element.14.dq_in, f32[8,4,32,128]{3,2,1,0:T(8,128)} %get-tuple-element.15.grad_t, s32[512,256]{1,0:T(8,128)} %m_codes.1, ...), custom_call_target="tpu_custom_call" | custom-call | tf_op jit(solution)/shard_map/adam/pallas_call | solution.py:582

commit v6 on v5

--- a/solution.py
+++ b/solution.py
@@ -557,9 +557,10 @@
     dq_in, grad_t, m_codes, m_scales, v_codes, v_scales, dq, update, m_norm, m_absmax, v_norm, v_absmax, grad
 ):
     dq[...] = dq_in[...]
-    grad[...] = grad_t[:, 0].reshape(256, 128).T
-    base = pl.program_id(0) * 16
-    for b in range(16):
+    for half in range(2):
+        grad[pl.ds(half * 128, 128), :] = grad_t[:, half].reshape(256, 128).T
+    base = pl.program_id(0) * 32
+    for b in range(32):
         rows = pl.ds(b * 8, 8)
         g = grad[rows, :]
         m = 0.9 * (m_codes[rows, :].astype(F32) * (m_scales[base + b] * (1.0 / 127.0))) + 0.1 * g
@@ -575,17 +576,17 @@
 
 def adam(dq, grad_t, m_codes, m_scales, v_codes, v_scales):
     smem = pl.BlockSpec(memory_space=pltpu.SMEM)
-    rows = pl.BlockSpec((128, 256), lambda q: (q, 0))
-    slab = pl.BlockSpec((dq.shape[0] // 4, dq.shape[1]), lambda q: (q, 0))
+    rows = pl.BlockSpec((256, 256), lambda q: (q, 0))
+    slab = pl.BlockSpec((dq.shape[0] // 2, dq.shape[1]), lambda q: (q, 0))
     big = jax.ShapeDtypeStruct(m_codes.shape, F32)
     small = jax.ShapeDtypeStruct(m_scales.shape, F32)
     return pl.pallas_call(
         adam_kernel,
-        grid=(4,),
+        grid=(2,),
         out_shape=[jax.ShapeDtypeStruct(dq.shape, dq.dtype), big, big, small, big, small],
-        in_specs=[slab, pl.BlockSpec((8, 1, 32, 128), lambda q: (0, q, 0, 0)), rows, smem, rows, smem],
+        in_specs=[slab, pl.BlockSpec((8, 2, 32, 128), lambda q: (0, q, 0, 0)), rows, smem, rows, smem],
         out_specs=[slab, rows, rows, smem, rows, smem],
-        scratch_shapes=[pltpu.VMEM((128, 256), F32)],
+        scratch_shapes=[pltpu.VMEM((256, 256), F32)],
         compiler_params=pltpu.CompilerParams(vmem_limit_bytes=60 * 2**20),
         name="adam",
     )(dq, grad_t, m_codes, m_scales, v_codes, v_scales)

time: 82.3 us -> 81.1 us (0.985)
  Pallas kernels: 81.5 us -> 80.3 us
    pallas_call x1, Pallas kernels: 4.34 us -> 3.19 us  [adam(): pl.pallas_call(adam_kernel, grid=(2,), out_shape=[jax.ShapeDtypeStruct(dq...]
where the time goes in v6:
time: 81.1 us; the launch traced here: 81 us
  Pallas kernels  80.3 us (99%)
    pallas_call x1, Pallas kernels, backward(): pl.pallas_call(backward_kernel, out_shape=[jax.ShapeDtypeStruct(queries.s...  77.2 us
    pallas_call x1, Pallas kernels, adam(): pl.pallas_call(adam_kernel, grid=(2,), out_shape=[jax.ShapeDtypeStruct(dq...  3.19 us

profile of v6, /device:TPU:8, one launch (start us, length us, event | category | flops | bytes accessed | tf_op | source)
XLA Modules:
  0.0 81.0 jit_solution(11959506891963174404)
XLA Ops:
  0.6 77.2 %backward.1 = (bf16[192,2048]{1,0:T(8,128)(2,1)}, f32[8,4,32,128]{3,2,1,0:T(8,128)}) custom-call(s32[16]{0:T(128)} %order.1, s32[1,8]{1,0:T(1,128)} %lens.1, bf16[192,2048]{1,0:T(8,128)(2,1)} %bitcast.7, bf16[192,2048]{1,0:T(8,128)(2,1)} %bitcast.8, bf16[192,128]{1,0:T(8,128)(2,1)} %bitcast.9, bf16[192,128]{1,0:T(8,128)(2,1)} %bitcast.10, ...), custom_call_target="tpu_custom_call" | custom-call | tf_op jit(solution)/shard_map/backward/pallas_call | solution.py:501
  77.8 3.2 %adam.1 = (bf16[192,2048]{1,0:T(8,128)(2,1)}, f32[512,256]{1,0:T(8,128)}, f32[512,256]{1,0:T(8,128)}, f32[64]{0:T(128)}, f32[512,256]{1,0:T(8,128)}, /*index=5*/f32[64]{0:T(128)}) custom-call(bf16[192,2048]{1,0:T(8,128)(2,1)} %get-tuple-element.14.dq_in, f32[8,4,32,128]{3,2,1,0:T(8,128)} %get-tuple-element.15.grad_t, s32[512,256]{1,0:T(8,128)} %m_codes.1, ...), custom_call_target="tpu_custom_call" | custom-call | tf_op jit(solution)/shard_map/adam/pallas_call | solution.py:583
